TPU v7x, 32 devices: a whole 2x2x4 slice. The times are simulated.
32 devices in a mesh: grp: 4 (over y, x), dp: 8 (over z, core).
Axes of the slice: x: 2, y: 2, z: 4, core: 2. Of those that a mesh axis runs over, the one named last changes fastest.
Arguments:
- source_ids: int32 [2, 32, 512], P(None, ('grp', 'dp')), may hold values from 0 to 32127
- target_inputs: int32 [2, 32, 256], P(None, ('grp', 'dp')), may hold values from 0 to 32127
- lengths: int32 [2, 32, 2], P(None, ('grp', 'dp')), may hold values from 64 to 512, as said below
- positions: int32 [2, 32, 256], P(None, ('grp', 'dp')), may hold values from 0 to 255, as said below
- target_ids: int32 [2, 32, 256], P(None, ('grp', 'dp')), may hold values from 0 to 32127
- target_mask: int32 [2, 32, 256], P(None, ('grp', 'dp')), may hold values from 0 to 1, as said below
- table: bfloat16 [32128, 512], P('dp')
- backbone_attn: bfloat16 [3, 512, 2048], replicated, may hold values from -0.25 to 0.25
- backbone_ffn_in: bfloat16 [2, 512, 2048], replicated, may hold values from -0.25 to 0.25
- backbone_ffn_out: bfloat16 [2, 2048, 512], replicated, may hold values from -0.125 to 0.125
- backbone_gains: float32 [6, 512], replicated, may hold values from 0.5 to 1.5
- inner_weights: float32 [4, 279104], P('grp')
- first_moment: float32 [4, 279104], P('grp'), may hold values from -3.0517578e-05 to 3.0517578e-05
- second_moment: float32 [4, 279104], P('grp'), may hold values from 3.6187227e-12 to 1.4474891e-11
- anchor: float32 [279104], replicated
- outer_momentum: float32 [279104], replicated, may hold values from -0.75 to 0.75
Outputs:
- loss_sum: float32 [4], P('grp')
- target_count: float32 [4], P('grp')
- grad_norm: float32 [4], P('grp')
- new_first: float32 [4, 279104], P('grp')
- new_second: float32 [4, 279104], P('grp')
- new_inner: float32 [4, 279104], P('grp')
- outer_delta: float32 [279104], replicated
- new_momentum: float32 [279104], replicated
- new_anchor: float32 [279104], replicated
Inputs may be any that keep to these rules, and one draw needn't show every extreme that they name: lengths[m, b, 0] is a source length of at least 128 and lengths[m, b, 1] a target length from 64 to 256; pair 0 of micro-batch 0 has both at 512 and 256. `positions`: each position is below its pair's target length. `target_mask`: the first entry of every pair's mask is 1.
All inputs are finite; a program needn't handle non-finite values.
Results may differ from a plain program's by a relative error of at most 0.0079.
Values may be sent and summed in bfloat16 or wider, within the bound.
No kernel may reach another device: no remote copies, remote signals or barrier semaphores. Data moves between devices by JAX's collectives and lax.ppermute only.
A program may use at most 320 MiB of HBM per device.

v0:
```python
import jax
import jax.numpy as jnp
from jax import lax
from jax.sharding import PartitionSpec as P

D = 512
HEADS = 8
SIDE = 64
SIDE_HEADS = 8
SIDE_FF = 256
STEP = 5


norm_eps = 1e-06
negative = -1000000000.0
beta_first = 0.9
beta_second = 0.99
adam_eps = 1e-08
learn_rate = 0.03
decay_rate = 0.01
clip_norm = 0.01
outer_rate = 0.7
outer_beta = 0.9


def matmul(left, right):
    return jnp.dot(left, right, preferred_element_type=jnp.float32)


def left_product(left, right):
    return lax.dot_general(
        left, right, (((0,), (0,)), ((), ())), preferred_element_type=jnp.float32
    )


def right_product(left, right):
    return lax.dot_general(
        left, right, (((1,), (1,)), ((), ())), preferred_element_type=jnp.float32
    )


def normalize(values, gain):
    return values * lax.rsqrt(jnp.mean(values * values, axis=-1, keepdims=True) + norm_eps) * gain


def norm_back(values, gain, grad):
    return jax.vjp(normalize, values, gain)[1](grad)


def gelu_tanh(values):
    return jax.nn.gelu(values, approximate=True)


def blend(logit, joined, late):
    gate = jax.nn.sigmoid(logit)
    return gate * joined + (1.0 - gate) * late


def layout():
    return [
        ("down", (4, D, SIDE)),
        ("attn_in", (3, SIDE, 3 * SIDE)),
        ("attn_out", (3, SIDE, SIDE)),
        ("ffn_in", (2, SIDE, SIDE_FF)),
        ("ffn_out", (2, SIDE_FF, SIDE)),
        ("upsample", (SIDE, D)),
        ("small", (9, SIDE)),
    ]


def unpack(flat):
    parts = {}
    offset = 0
    for label, shape in layout():
        count = 1
        for extent in shape:
            count = count * extent
        parts[label] = flat[offset : offset + count].reshape(shape)
        offset = offset + count
    return parts


def allowed_keys(block, keys, valid, causal):
    key_pos = jnp.arange(keys)
    allowed = jnp.broadcast_to(key_pos[None, :] < valid, (block, keys))
    if causal:
        allowed = allowed & (key_pos[None, :] <= jnp.arange(block)[:, None])
    return allowed


def attend(query_b, keys_b, values_b, heads, valid, causal):
    length = query_b.shape[0]
    size = query_b.shape[1] // heads
    block = min(512, length)
    key_heads = keys_b.reshape(-1, heads, size)
    value_heads = values_b.reshape(-1, heads, size)
    query_heads = query_b.reshape(block, heads, size)
    scores = jnp.einsum(
        "qhd,khd->hqk", query_heads, key_heads, preferred_element_type=jnp.float32
    ) * size ** (-0.5)
    scores = jnp.where(allowed_keys(block, keys_b.shape[0], valid, causal)[None], scores, negative)
    peak = jnp.max(scores, axis=-1, keepdims=True)
    shifted = jnp.exp(scores - peak)
    total = jnp.sum(shifted, axis=-1, keepdims=True)
    mixing = (shifted / total).astype(jnp.bfloat16)
    outputs = jnp.einsum(
        "hqk,khd->qhd", mixing, value_heads, preferred_element_type=jnp.float32
    ).reshape(block, -1)
    totals = (peak + jnp.log(total))[..., 0]
    return (outputs, totals)


def attend_back(query_b, keys_b, values_b, totals, grad_b, heads, valid, causal):
    length = query_b.shape[0]
    size = query_b.shape[1] // heads
    block = min(512, length)
    scale = size ** (-0.5)
    key_heads = keys_b.reshape(-1, heads, size)
    value_heads = values_b.reshape(-1, heads, size)
    query_heads = query_b.reshape(block, heads, size)
    grad_heads = grad_b.reshape(block, heads, size)
    scores = (
        jnp.einsum("qhd,khd->hqk", query_heads, key_heads, preferred_element_type=jnp.float32)
        * scale
    )
    scores = jnp.where(allowed_keys(block, keys_b.shape[0], valid, causal)[None], scores, negative)
    mixing = jnp.exp(scores - totals[:, 0:block, None])
    grad_values = jnp.einsum(
        "hqk,qhd->khd", mixing.astype(jnp.bfloat16), grad_heads, preferred_element_type=jnp.float32
    )
    grad_mixing = (
        jnp.einsum("qhd,khd->hqk", grad_heads, value_heads, preferred_element_type=jnp.float32)
        .astype(jnp.bfloat16)
        .astype(jnp.float32)
    )
    grad_scores = (
        mixing * (grad_mixing - jnp.sum(grad_mixing * mixing, axis=-1, keepdims=True))
    ).astype(jnp.bfloat16)
    grad_query = (
        jnp.einsum(
            "hqk,khd->qhd", grad_scores, key_heads, preferred_element_type=jnp.float32
        ).reshape(block, -1)
        * scale
    )
    grad_keys = (
        jnp.einsum("hqk,qhd->khd", grad_scores, query_heads, preferred_element_type=jnp.float32)
        * scale
    )
    width = heads * size
    return (grad_query, grad_keys.reshape(-1, width), grad_values.reshape(-1, width))


def frozen_attention(normed_b, source_b, weight, valid, causal):
    query_b = matmul(normed_b, weight[:, :D]).astype(jnp.bfloat16)
    keyval_b = matmul(source_b, weight[:, D : 3 * D]).astype(jnp.bfloat16)
    mixed, totals = attend(query_b, keyval_b[:, :D], keyval_b[:, D:], HEADS, valid, causal)
    return matmul(mixed.astype(jnp.bfloat16), weight[:, 3 * D :])


def frozen_ffn(normed, weight_in, weight_out):
    hidden = gelu_tanh(matmul(normed.astype(jnp.bfloat16), weight_in))
    return matmul(hidden.astype(jnp.bfloat16), weight_out)


def backbone(embed_src, embed_tgt, src_len, tgt_len, attn, ffn_in, ffn_out, gains):
    state = embed_src.astype(jnp.float32)
    normed_b = normalize(state, gains[0]).astype(jnp.bfloat16)
    state = state + frozen_attention(normed_b, normed_b, attn[0], src_len, False)
    state = state + frozen_ffn(normalize(state, gains[1]), ffn_in[0], ffn_out[0])
    encoded = normalize(state, gains[2]).astype(jnp.bfloat16)
    flow = embed_tgt.astype(jnp.float32)
    normed_b = normalize(flow, gains[3]).astype(jnp.bfloat16)
    flow = flow + frozen_attention(normed_b, normed_b, attn[1], tgt_len, True)
    flow = flow + frozen_attention(
        normalize(flow, gains[4]).astype(jnp.bfloat16), encoded, attn[2], src_len, False
    )
    flow = flow + frozen_ffn(normalize(flow, gains[5]), ffn_in[1], ffn_out[1])
    return (encoded, flow.astype(jnp.bfloat16))


def side_attend(normed_b, source_b, weight_in, weight_out, valid, causal):
    w_in_b = weight_in.astype(jnp.bfloat16)
    query_b = matmul(normed_b, w_in_b[:, :SIDE]).astype(jnp.bfloat16)
    keyval_b = matmul(source_b, w_in_b[:, SIDE:]).astype(jnp.bfloat16)
    mixed, totals = attend(
        query_b, keyval_b[:, :SIDE], keyval_b[:, SIDE:], SIDE_HEADS, valid, causal
    )
    mixed_b = mixed.astype(jnp.bfloat16)
    return (
        matmul(mixed_b, weight_out.astype(jnp.bfloat16)),
        (normed_b, source_b, query_b, keyval_b, mixed_b, totals),
    )


def side_attend_back(kept, weight_in, weight_out, grad_out, valid, causal):
    normed_b, source_b, query_b, keyval_b, mixed_b, totals = kept
    grad_b = grad_out.astype(jnp.bfloat16)
    w_in_b = weight_in.astype(jnp.bfloat16)
    grad_w_out = left_product(mixed_b, grad_b)
    grad_mixed = right_product(grad_b, weight_out.astype(jnp.bfloat16)).astype(jnp.bfloat16)
    grad_query, grad_keys, grad_values = attend_back(
        query_b,
        keyval_b[:, :SIDE],
        keyval_b[:, SIDE:],
        totals,
        grad_mixed,
        SIDE_HEADS,
        valid,
        causal,
    )
    grad_query_b = grad_query.astype(jnp.bfloat16)
    grad_keyval_b = jnp.concatenate([grad_keys, grad_values], axis=1).astype(jnp.bfloat16)
    grad_normed = right_product(grad_query_b, w_in_b[:, :SIDE])
    grad_source = right_product(grad_keyval_b, w_in_b[:, SIDE:])
    grad_w_in = jnp.concatenate(
        [left_product(normed_b, grad_query_b), left_product(source_b, grad_keyval_b)], axis=1
    )
    return (grad_normed, grad_source, grad_w_in, grad_w_out)


def side_ffn(normed_b, weight_in, weight_out):
    hidden = matmul(normed_b, weight_in.astype(jnp.bfloat16))
    active_b = gelu_tanh(hidden).astype(jnp.bfloat16)
    return (matmul(active_b, weight_out.astype(jnp.bfloat16)), (normed_b, hidden, active_b))


def side_ffn_back(kept, weight_in, weight_out, grad_out):
    normed_b, hidden, active_b = kept
    grad_b = grad_out.astype(jnp.bfloat16)
    grad_w_out = left_product(active_b, grad_b)
    grad_active = right_product(grad_b, weight_out.astype(jnp.bfloat16))
    grad_hidden = jax.vjp(gelu_tanh, hidden)[1](grad_active)[0].astype(jnp.bfloat16)
    return (
        right_product(grad_hidden, weight_in.astype(jnp.bfloat16)),
        left_product(normed_b, grad_hidden),
        grad_w_out,
    )


def side_forward(parts, embed_src, encoded, embed_tgt, decoded, src_len, tgt_len):
    small = parts["small"]
    down_b = parts["down"].astype(jnp.bfloat16)
    kept = {}
    kept["enc_start"] = matmul(embed_src, down_b[0])
    normed_b = normalize(kept["enc_start"], small[0]).astype(jnp.bfloat16)
    branch, kept["enc_attn"] = side_attend(
        normed_b, normed_b, parts["attn_in"][0], parts["attn_out"][0], src_len, False
    )
    kept["enc_mid"] = kept["enc_start"] + branch
    branch, kept["enc_ffn"] = side_ffn(
        normalize(kept["enc_mid"], small[1]).astype(jnp.bfloat16),
        parts["ffn_in"][0],
        parts["ffn_out"][0],
    )
    kept["enc_late"] = kept["enc_mid"] + branch
    kept["enc_joined"] = matmul(encoded, down_b[1])
    kept["enc_final"] = blend(small[7], kept["enc_joined"], kept["enc_late"])
    memory_b = normalize(kept["enc_final"], small[2]).astype(jnp.bfloat16)
    kept["dec_start"] = matmul(embed_tgt, down_b[2])
    normed_b = normalize(kept["dec_start"], small[3]).astype(jnp.bfloat16)
    branch, kept["dec_attn"] = side_attend(
        normed_b, normed_b, parts["attn_in"][1], parts["attn_out"][1], tgt_len, True
    )
    kept["dec_one"] = kept["dec_start"] + branch
    branch, kept["cross_attn"] = side_attend(
        normalize(kept["dec_one"], small[4]).astype(jnp.bfloat16),
        memory_b,
        parts["attn_in"][2],
        parts["attn_out"][2],
        src_len,
        False,
    )
    kept["dec_two"] = kept["dec_one"] + branch
    branch, kept["dec_ffn"] = side_ffn(
        normalize(kept["dec_two"], small[5]).astype(jnp.bfloat16),
        parts["ffn_in"][1],
        parts["ffn_out"][1],
    )
    kept["dec_three"] = kept["dec_two"] + branch
    kept["dec_joined"] = matmul(decoded, down_b[3])
    kept["dec_final"] = blend(small[8], kept["dec_joined"], kept["dec_three"])
    return (normalize(kept["dec_final"], small[6]), kept)


def side_backward(
    parts, kept, grad_top, grad_up, embed_src, encoded, embed_tgt, decoded, src_len, tgt_len
):
    small = parts["small"]
    attn_in = parts["attn_in"]
    attn_out = parts["attn_out"]
    grad_final, gain_six = norm_back(kept["dec_final"], small[6], grad_top)
    logit_eight, grad_joined, grad_three = jax.vjp(
        blend, small[8], kept["dec_joined"], kept["dec_three"]
    )[1](grad_final)
    down_three = left_product(decoded, grad_joined.astype(jnp.bfloat16))
    grad_normed, ffn_in_one, ffn_out_one = side_ffn_back(
        kept["dec_ffn"], parts["ffn_in"][1], parts["ffn_out"][1], grad_three
    )
    part_two, gain_five = norm_back(kept["dec_two"], small[5], grad_normed)
    grad_two = grad_three + part_two
    grad_normed, grad_memory, in_two, out_two = side_attend_back(
        kept["cross_attn"], attn_in[2], attn_out[2], grad_two, src_len, False
    )
    part_one, gain_four = norm_back(kept["dec_one"], small[4], grad_normed)
    grad_one = grad_two + part_one
    grad_normed, grad_source, in_one, out_one = side_attend_back(
        kept["dec_attn"], attn_in[1], attn_out[1], grad_one, tgt_len, True
    )
    part_start, gain_three = norm_back(kept["dec_start"], small[3], grad_normed + grad_source)
    down_two = left_product(embed_tgt, (grad_one + part_start).astype(jnp.bfloat16))
    grad_enc_final, gain_two = norm_back(kept["enc_final"], small[2], grad_memory)
    logit_seven, grad_enc_joined, grad_late = jax.vjp(
        blend, small[7], kept["enc_joined"], kept["enc_late"]
    )[1](grad_enc_final)
    down_one = left_product(encoded, grad_enc_joined.astype(jnp.bfloat16))
    grad_normed, ffn_in_zero, ffn_out_zero = side_ffn_back(
        kept["enc_ffn"], parts["ffn_in"][0], parts["ffn_out"][0], grad_late
    )
    part_mid, gain_one = norm_back(kept["enc_mid"], small[1], grad_normed)
    grad_mid = grad_late + part_mid
    grad_normed, grad_source, in_zero, out_zero = side_attend_back(
        kept["enc_attn"], attn_in[0], attn_out[0], grad_mid, src_len, False
    )
    part_start, gain_zero = norm_back(kept["enc_start"], small[0], grad_normed + grad_source)
    down_zero = left_product(embed_src, (grad_mid + part_start).astype(jnp.bfloat16))
    pieces = [
        jnp.stack([down_zero, down_one, down_two, down_three]),
        jnp.stack([in_zero, in_one, in_two]),
        jnp.stack([out_zero, out_one, out_two]),
        jnp.stack([ffn_in_zero, ffn_in_one]),
        jnp.stack([ffn_out_zero, ffn_out_one]),
        grad_up,
        jnp.stack(
            [
                gain_zero,
                gain_one,
                gain_two,
                gain_three,
                gain_four,
                gain_five,
                gain_six,
                logit_seven,
                logit_eight,
            ]
        ),
    ]
    return jnp.concatenate([piece.reshape(-1) for piece in pieces])


def vocab_head(head_in, targets, weights, table_rows):
    logits = right_product(head_in, table_rows)
    peak = jnp.max(logits, axis=1, keepdims=True)
    log_total = peak[:, 0] + jnp.log(jnp.sum(jnp.exp(logits - peak), axis=1))
    hit = jnp.arange(logits.shape[1])[None, :] == targets[:, None]
    target_logit = jnp.sum(jnp.where(hit, logits, 0.0), axis=1)
    loss_sum = jnp.sum(weights * (log_total - target_logit))
    grad_logits = (jnp.exp(logits - log_total[:, None]) - hit.astype(jnp.float32)).astype(
        jnp.bfloat16
    )
    grad_in = matmul(grad_logits, table_rows)
    return (loss_sum, grad_in * weights[:, None])


def per_device(
    source_ids,
    target_inputs,
    lengths,
    positions,
    target_ids,
    target_mask,
    table,
    backbone_attn,
    backbone_ffn_in,
    backbone_ffn_out,
    backbone_gains,
    inner_weights,
    first_moment,
    second_moment,
    anchor,
    outer_momentum,
):
    micro = source_ids.shape[0]
    src_tokens = source_ids.shape[2]
    tgt_tokens = target_inputs.shape[2]
    id_list = jnp.concatenate([source_ids.reshape(-1), target_inputs.reshape(-1)])
    table_rows = lax.all_gather(table, "dp", axis=0, tiled=True)
    embedded = jnp.take(table_rows, id_list, axis=0)
    target_table = target_ids[:, 0]
    parts = unpack(inner_weights[0])
    up_b = parts["upsample"].astype(jnp.bfloat16)
    grad_total = jnp.zeros(inner_weights.shape[1:], jnp.float32)
    loss_total = jnp.zeros((), jnp.float32)
    count_total = jnp.zeros((), jnp.float32)
    for index in range(micro):
        embed_src = embedded[index * src_tokens : (index + 1) * src_tokens]
        base = micro * src_tokens + index * tgt_tokens
        embed_tgt = embedded[base : base + tgt_tokens]
        src_len = lengths[index, 0, 0]
        tgt_len = lengths[index, 0, 1]
        encoded, decoded = backbone(
            embed_src,
            embed_tgt,
            src_len,
            tgt_len,
            backbone_attn,
            backbone_ffn_in,
            backbone_ffn_out,
            backbone_gains,
        )
        top, kept = side_forward(parts, embed_src, encoded, embed_tgt, decoded, src_len, tgt_len)
        picks = positions[index, 0]
        picked_b = jnp.take(top, picks, axis=0).astype(jnp.bfloat16)
        head_in = (matmul(picked_b, up_b) * D ** (-0.5)).astype(jnp.bfloat16)
        weights = target_mask[index, 0].astype(jnp.float32)
        loss_sum, grad_head = vocab_head(head_in, target_table[index], weights, table_rows)
        grad_lifted = (grad_head * D ** (-0.5)).astype(jnp.bfloat16)
        grad_up = left_product(picked_b, grad_lifted)
        grad_top = jnp.zeros(top.shape, jnp.float32).at[picks].add(right_product(grad_lifted, up_b))
        flat = side_backward(
            parts, kept, grad_top, grad_up, embed_src, encoded, embed_tgt, decoded, src_len, tgt_len
        )
        count = jnp.sum(weights)
        grad_total = grad_total + flat
        loss_total = loss_total + loss_sum
        count_total = count_total + count
    grad_total, loss_total, count_total = lax.psum((grad_total, loss_total, count_total), "dp")
    mean_grad = grad_total / count_total
    norm = jnp.sqrt(jnp.sum(mean_grad * mean_grad))
    clipped = mean_grad * jnp.minimum(1.0, clip_norm / norm)
    moment_one = beta_first * first_moment[0] + (1.0 - beta_first) * clipped
    moment_two = beta_second * second_moment[0] + (1.0 - beta_second) * clipped * clipped
    fixed_one = moment_one / (1.0 - beta_first**STEP)
    fixed_two = moment_two / (1.0 - beta_second**STEP)
    old_weights = inner_weights[0]
    new_inner = old_weights - learn_rate * (
        fixed_one / (jnp.sqrt(fixed_two) + adam_eps) + decay_rate * old_weights
    )
    delta = lax.psum(anchor - new_inner, "grp") / lax.axis_size("grp")
    momentum = outer_beta * outer_momentum + delta
    new_anchor = anchor - outer_rate * (delta + outer_beta * momentum)
    return (
        loss_total[None],
        count_total[None],
        norm[None],
        moment_one[None],
        moment_two[None],
        new_inner[None],
        delta,
        momentum,
        new_anchor,
    )


def solution(mesh):
    return jax.shard_map(
        per_device,
        mesh=mesh,
        in_specs=(
            P(None, ("grp", "dp"), None),
            P(None, ("grp", "dp"), None),
            P(None, ("grp", "dp"), None),
            P(None, ("grp", "dp"), None),
            P(None, ("grp", "dp"), None),
            P(None, ("grp", "dp"), None),
            P("dp", None),
            P(),
            P(),
            P(),
            P(),
            P("grp", None),
            P("grp", None),
            P("grp", None),
            P(),
            P(),
        ),
        out_specs=(
            P("grp"),
            P("grp"),
            P("grp"),
            P("grp", None),
            P("grp", None),
            P("grp", None),
            P(),
            P(),
            P(),
        ),
        check_vma=False,
    )
```

profile of v0, /device:TPU:9, one launch (start us, length us, event | category | flops | bytes accessed | tf_op | source)
XLA Modules:
  0.0 817.2 jit_solution(9297667034356502082)
XLA Ops:
  8.4 11.0 %fusion.536 = (f32[279104]{0:T(1024)}, bf16[1,279104]{1,0:T(2,128)(2,1)S(1)}) fusion(f32[1,279104]{1,0:T(1,128)S(1)} %copy-done.42), kind=kLoop, calls=%fused_computation.921 | loop fusion | flops 279104 | bytes 2791040 | tf_op args[11]
  41.3 5.8 slice_bitcast_fusion
  47.1 244.4 %all-gather.2.cloned.1.call-done = bf16[32128,512]{1,0:T(8,128)(2,1)} async-done(((bf16[4016,512]{1,0:T(8,128)(2,1)}), bf16[32128,512]{1,0:T(8,128)(2,1)}) %all-gather.2.cloned.1.call-update) | async-done | bytes 32899088 | tf_op jit(solution)/shard_map/all_gather | solution.py:386
  291.5 9.9 %gather_fusion = bf16[1536,512]{1,0:T(8,128)(2,1)S(1)} fusion(bf16[32128,512]{1,0:T(8,128)(2,1)} %all-gather.2.cloned.1.call-done, s32[2048]{0:T(1024)S(1)} %pad_clamp_fusion), kind=kCustom, calls=%fused_computation.2 | custom fusion | bytes 3151872 | tf_op jit(solution)/shard_map/jit(_take)/gather | solution.py:387
  329.7 7.7 fusion.552
  337.4 4.2 fusion.151
  344.1 6.4 multiply_reduce_fusion.5
  353.6 7.9 fusion.549
  361.5 4.2 fusion.150
  368.3 6.6 multiply_reduce_fusion.3
  407.2 4.6 fusion.562
  411.9 3.1 fusion.171
  436.6 3.5 fusion.558
  440.1 3.1 fusion.170
  444.7 3.8 fusion.165
  448.8 3.9 fusion.162
  455.3 23.3 %fusion.563 = (f32[256]{0:T(256)S(1)}, f32[256,32128]{1,0:T(8,128)}) fusion(bf16[32128,512]{1,0:T(8,128)(2,1)} %all-gather.2.cloned.1.call-done, bf16[64,512]{1,0:T(8,128)(2,1)S(1)} %convert_element_type.768, bf16[256,64]{1,0:T(8,128)(2,1)S(1)} %gather_fusion.1, pred[256]{0:T(512)(128)(4,1)S(1)} %copy-done.170), kind=kOutput, calls=%fused_computation.944 | convolution fusion | flops 8447442944 | bytes 65897728 | tf_op jit(solution)/shard_map/dot_general | solution.py:37
  478.6 16.4 %select_reduce_fusion.1 = (f32[256]{0:T(256)S(1)}, f32[256]{0:T(256)S(1)}) fusion(f32[256,32128]{1,0:T(8,128)} %get-tuple-element.251, s32[256]{0:T(256)S(1)} %bitcast.644, f32[256]{0:T(256)S(1)} %get-tuple-element.250), kind=kLoop, calls=%fused_computation.16 | loop fusion | flops 41123328 | bytes 32903168 | tf_op jit(solution)/shard_map/reduce_sum | solution.py:355
  495.6 23.2 %fusion.173 = bf16[256,512]{1,0:T(8,128)(2,1)S(1)} fusion(bf16[32128,512]{1,0:T(8,128)(2,1)} %all-gather.2.cloned.1.call-done, f32[256,32128]{1,0:T(8,128)} %get-tuple-element.251, f32[256]{0:T(256)S(1)} %get-tuple-element.91, s32[256]{0:T(256)S(1)} %bitcast.645, f32[256]{0:T(256)S(1)} %bitcast.653), kind=kOutput, calls=%fused_computation.257 | convolution fusion | flops 8463679488 | bytes 66063360 | tf_op jit(solution)/shard_map/dot_general | solution.py:27
  521.9 23.6 %fusion.564 = (f32[256]{0:T(256)S(1)}, f32[256,32128]{1,0:T(8,128)}) fusion(bf16[32128,512]{1,0:T(8,128)(2,1)} %all-gather.2.cloned.1.call-done, bf16[64,512]{1,0:T(8,128)(2,1)S(1)} %convert_element_type.768, bf16[256,64]{1,0:T(8,128)(2,1)S(1)} %gather_fusion.2, pred[256]{0:T(512)(128)(4,1)S(1)} %copy-done.172), kind=kOutput, calls=%fused_computation.945 | convolution fusion | flops 8447442944 | bytes 65897728 | tf_op jit(solution)/shard_map/dot_general | solution.py:37
  545.4 16.1 %select_reduce_fusion = (f32[256]{0:T(256)S(1)}, f32[256]{0:T(256)S(1)}) fusion(f32[256,32128]{1,0:T(8,128)} %get-tuple-element.253, s32[256]{0:T(256)S(1)} %bitcast.642, f32[256]{0:T(256)S(1)} %get-tuple-element.252), kind=kLoop, calls=%fused_computation.13 | loop fusion | flops 41123328 | bytes 32903168 | tf_op jit(solution)/shard_map/reduce_sum | solution.py:355
  562.3 23.2 %fusion.172 = bf16[256,512]{1,0:T(8,128)(2,1)S(1)} fusion(bf16[32128,512]{1,0:T(8,128)(2,1)} %all-gather.2.cloned.1.call-done, f32[256,32128]{1,0:T(8,128)} %get-tuple-element.253, f32[256]{0:T(256)S(1)} %get-tuple-element.85, s32[256]{0:T(256)S(1)} %bitcast.643, f32[256]{0:T(256)S(1)} %bitcast.651), kind=kOutput, calls=%fused_computation.256 | convolution fusion | flops 8463679488 | bytes 66063360 | tf_op jit(solution)/shard_map/dot_general | solution.py:27
  685.7 14.2 %multiply_reduce_fusion.1 = (f32[279104]{0:T(1024)S(1)}, f32[279104]{0:T(1024)}) fusion(f32[1,279104]{1,0:T(1,128)} %param.31, f32[1,279104]{1,0:T(1,128)} %param.30), kind=kLoop, calls=%fused_computation.368 | loop fusion | flops 558208 | bytes 4465664 | tf_op jit(solution)/shard_map/mul | solution.py:431
  701.2 13.6 %all-reduce = (f32[1]{0:T(128)}, f32[]{:T(128)}) all-reduce(f32[1]{0:T(128)} %bitcast.98, f32[]{:T(128)S(6)} %add.670), channel_id=1, replica_groups=mesh['grp'=4,'dp'=8] {'dp'}, use_global_device_ids=true, to_apply=%region_58.60 | all-reduce | flops 2 | bytes 16 | tf_op jit(solution)/shard_map/psum | solution.py:426
  714.7 26.9 %all-reduce.4.cloned.1.call-done = f32[279104]{0:T(1024)} async-done(((f32[279104]{0:T(1024)}), f32[279104]{0:T(1024)}) %all-reduce.4.cloned.1.call-update) | async-done | bytes 1116432 | tf_op jit(solution)/shard_map/psum | solution.py:426
  741.7 2.8 multiply_reduce_fusion
  745.2 4.9 fusion.534
  750.2 6.0 broadcast_in_dim.201
  756.2 5.9 broadcast_in_dim.202
  762.1 5.9 broadcast_in_dim.203
  768.0 37.8 %all-reduce.6.cloned.1.call-done = f32[279104]{0:T(1024)} async-done(((f32[279104]{0:T(1024)}), f32[279104]{0:T(1024)}) %all-reduce.6.cloned.1.call-update) | async-done | bytes 1116432 | tf_op jit(solution)/shard_map/psum | solution.py:438
  805.8 3.2 multiply_subtract_fusion
  (1005 shorter events, 216.9 us)
Async XLA Ops:
  7.2 284.4 %all-gather.2.cloned.1.call-start = ((), (), s32[]{:S(2)}) async-start(), calls=%async_computation | async-start | bytes 37011456 | tf_op jit(solution)/shard_map/all_gather | solution.py:386
  7.9 733.8 %all-reduce.4.cloned.1.call-start = ((), (), s32[]{:S(2)}) async-start(), calls=%async_computation.1 | async-start | bytes 2236416 | tf_op jit(solution)/shard_map/psum | solution.py:426
  19.5 18.0 %copy-start.311 = (s32[2,1,256]{2,1,0:T(1,128)S(1)}, s32[2,1,256]{2,1,0:T(1,128)}, u32[]{:S(2)}) copy-start(s32[2,1,256]{2,1,0:T(1,128)} %param.22) | copy-start | bytes 6148
  19.5 18.6 %copy-start.274 = (s32[2,1,256]{2,1,0:T(1,128)S(1)}, s32[2,1,256]{2,1,0:T(1,128)}, u32[]{:S(2)}) copy-start(s32[2,1,256]{2,1,0:T(1,128)} %param.23) | copy-start | bytes 6148
  19.5 19.8 %copy-start.265 = (f32[6,512]{1,0:T(8,128)S(1)}, f32[6,512]{1,0:T(8,128)}, u32[]{:S(2)}) copy-start(f32[6,512]{1,0:T(8,128)} %param.28) | copy-start | bytes 36868
  22.6 281.6 %copy-start.80 = (bf16[64,192]{1,0:T(8,128)(2,1)}, bf16[64,192]{1,0:T(8,128)(2,1)S(1)}, u32[]{:S(2)}) copy-start(bf16[64,192]{1,0:T(8,128)(2,1)S(1)} %convert_element_type.739) | copy-start | bytes 73732
  27.8 390.7 %copy-start.117 = (bf16[64,64]{1,0:T(8,128)(2,1)}, bf16[64,64]{1,0:T(8,128)(2,1)S(1)}, u32[]{:S(2)}) copy-start(bf16[64,64]{1,0:T(8,128)(2,1)S(1)} %convert_element_type.737) | copy-start | bytes 24580
  39.3 264.0 %copy-start.247 = (f32[64]{0:T(128)}, f32[64]{0:T(128)S(1)}, u32[]{:S(2)}) copy-start(f32[64]{0:T(128)S(1)} %get-tuple-element.110) | copy-start | bytes 772
  302.4 130.9 %copy-start.10 = (bf16[1536,512]{1,0:T(8,128)(2,1)}, bf16[1536,512]{1,0:T(8,128)(2,1)S(1)}, u32[]{:S(2)}) copy-start(bf16[1536,512]{1,0:T(8,128)(2,1)S(1)} %broadcast_select_fusion) | copy-start | bytes 4718596
  302.7 24.5 %copy-start.25 = (f32[512,64]{0,1:T(8,128)}, f32[512,64]{0,1:T(8,128)S(1)}, u32[]{:S(2)}) copy-start(f32[512,64]{0,1:T(8,128)S(1)} %get-tuple-element.199) | copy-start | bytes 393220
  304.2 18.7 %copy-start.64 = (bf16[512,128]{0,1:T(8,128)(2,1)}, bf16[512,128]{0,1:T(8,128)(2,1)S(1)}, u32[]{:S(2)}) copy-start(bf16[512,128]{0,1:T(8,128)(2,1)S(1)} %convolution_convert_fusion.23) | copy-start | bytes 393220
  310.4 108.1 %copy-start.38 = (f32[256,64]{0,1:T(8,128)}, f32[256,64]{0,1:T(8,128)S(1)}, u32[]{:S(2)}) copy-start(f32[256,64]{0,1:T(8,128)S(1)} %get-tuple-element.191) | copy-start | bytes 196612
  310.6 71.1 %copy-start.40 = (f32[256,64]{0,1:T(8,128)}, f32[256,64]{0,1:T(8,128)S(1)}, u32[]{:S(2)}) copy-start(f32[256,64]{0,1:T(8,128)S(1)} %get-tuple-element.189) | copy-start | bytes 196612
  311.3 78.3 %copy-start.76 = (bf16[256,64]{0,1:T(8,128)(2,1)}, bf16[256,64]{0,1:T(8,128)(2,1)S(1)}, u32[]{:S(2)}) copy-start(bf16[256,64]{0,1:T(8,128)(2,1)S(1)} %get-tuple-element.187) | copy-start | bytes 98308
  311.6 68.2 %copy-start.112 = (bf16[256,128]{0,1:T(8,128)(2,1)}, bf16[256,128]{0,1:T(8,128)(2,1)S(1)}, u32[]{:S(2)}) copy-start(bf16[256,128]{0,1:T(8,128)(2,1)S(1)} %convolution_convert_fusion.27) | copy-start | bytes 196612
  311.8 67.9 %copy-start.123 = (bf16[256,8,8]{0,2,1:T(8,128)(2,1)}, bf16[256,8,8]{0,2,1:T(8,128)(2,1)S(1)}, u32[]{:S(2)}) copy-start(bf16[256,8,8]{0,2,1:T(8,128)(2,1)S(1)} %fusion.236) | copy-start | bytes 98308
  318.9 59.3 %copy-start.23 = (f32[512,64]{0,1:T(8,128)}, f32[512,64]{0,1:T(8,128)S(1)}, u32[]{:S(2)}) copy-start(f32[512,64]{0,1:T(8,128)S(1)} %get-tuple-element.203) | copy-start | bytes 393220
  327.4 50.4 %copy-start.21 = (f32[512,64]{0,1:T(8,128)}, f32[512,64]{0,1:T(8,128)S(1)}, u32[]{:S(2)}) copy-start(f32[512,64]{0,1:T(8,128)S(1)} %get-tuple-element.219) | copy-start | bytes 393220
  376.4 15.6 %copy-start.15 = (bf16[512,512]{1,0:T(8,128)(2,1)}, bf16[512,512]{1,0:T(8,128)(2,1)S(1)}, u32[]{:S(2)}) copy-start(bf16[512,512]{1,0:T(8,128)(2,1)S(1)} %get-tuple-element.140) | copy-start | bytes 1572868
  396.4 56.5 %copy-start.209 = (f32[256]{0:T(256)}, f32[256]{0:T(256)S(1)}, u32[]{:S(2)}) copy-start(f32[256]{0:T(256)S(1)} %fusion.482) | copy-start | bytes 3076
  425.0 166.3 %copy-start.212 = (f32[256]{0:T(256)}, f32[256]{0:T(256)S(1)}, u32[]{:S(2)}) copy-start(f32[256]{0:T(256)S(1)} %fusion.478) | copy-start | bytes 3076
  452.7 25.9 %copy-start.54 = (bf16[256,512]{1,0:T(8,128)(2,1)}, bf16[256,512]{1,0:T(8,128)(2,1)S(1)}, u32[]{:S(2)}) copy-start(bf16[256,512]{1,0:T(8,128)(2,1)S(1)} %fusion.162) | copy-start | bytes 786436
  455.3 23.4 %copy-start.32 = (bf16[256,64]{1,0:T(8,128)(2,1)}, bf16[256,64]{1,0:T(8,128)(2,1)S(1)}, u32[]{:S(2)}) copy-start(bf16[256,64]{1,0:T(8,128)(2,1)S(1)} %gather_fusion.1) | copy-start | bytes 98308
  455.3 23.3 %copy-start.284 = (s32[1,1,256]{2,1,0:T(1,128)S(1)}, s32[1,1,256]{2,1,0:T(1,128)}, u32[]{:S(2)}) copy-start(s32[1,1,256]{2,1,0:T(1,128)} %get-tuple-element.137) | copy-start | bytes 3076
  478.6 16.4 %copy-start.287 = (f32[1,1,256]{2,1,0:T(1,128)S(1)}, f32[1,1,256]{2,1,0:T(1,128)}, u32[]{:S(2)}) copy-start(f32[1,1,256]{2,1,0:T(1,128)} %get-tuple-element.143) | copy-start | bytes 3076
  495.6 26.2 %copy-start.172 = (pred[256]{0:T(512)(128)(4,1)S(1)}, pred[256]{0:T(512)(128)(4,1)}, u32[]{:S(2)}) copy-start(pred[256]{0:T(512)(128)(4,1)} %compare_and_fusion.1) | copy-start | bytes 772
  521.8 23.6 %copy-start.283 = (s32[1,1,256]{2,1,0:T(1,128)S(1)}, s32[1,1,256]{2,1,0:T(1,128)}, u32[]{:S(2)}) copy-start(s32[1,1,256]{2,1,0:T(1,128)} %get-tuple-element.136) | copy-start | bytes 3076
  545.4 16.2 %copy-start.286 = (f32[1,1,256]{2,1,0:T(1,128)S(1)}, f32[1,1,256]{2,1,0:T(1,128)}, u32[]{:S(2)}) copy-start(f32[1,1,256]{2,1,0:T(1,128)} %get-tuple-element.142) | copy-start | bytes 3076
  683.7 122.1 %all-reduce.6.cloned.1.call-start = ((), (), s32[]{:S(2)}) async-start(), calls=%async_computation.2 | async-start | bytes 2236416 | tf_op jit(solution)/shard_map/psum | solution.py:438
  685.7 59.5 %copy-start.17 = (f32[279104]{0:T(1024)S(1)}, f32[279104]{0:T(1024)}, u32[]{:S(2)}) copy-start(f32[279104]{0:T(1024)} %param.32) | copy-start | bytes 3349252
  685.7 59.5 %copy-start.18 = (f32[279104]{0:T(1024)S(1)}, f32[279104]{0:T(1024)}, u32[]{:S(2)}) copy-start(f32[279104]{0:T(1024)} %get-tuple-element.103) | copy-start | bytes 3349252
  756.2 49.7 %copy-start.51 = (f32[279104]{0:T(1024)S(1)}, f32[279104]{0:T(1024)}, u32[]{:S(2)}) copy-start(f32[279104]{0:T(1024)} %param.33) | copy-start | bytes 3349252
  (294 other events, 1250.0 us)
Sparse Core Ops, SparseCore 0:
  9.7 281.8 all-gather.1
  683.8 57.8 all-reduce.3
  750.3 55.4 all-reduce.5
where the time goes:
time: 828 us; the launch traced here: 817 us
  waiting for transfers between devices  310 us (37%)
  matrix products  270 us (33%)
  other arithmetic  112 us (14%)
  local copies, waits for them, and re-layouts  88.4 us (11%)
  between operations  23 us (3%)
  blocking collectives  13.6 us (2%)
    all_gather x1, waiting for transfers between devices, per_device(): table_rows = lax.all_gather(table, 'dp', axis=0, tiled=True)  244 us
    dot_general x58, matrix products, matmul(): return jnp.dot(left, right, preferred_element_type=jnp.float32)  104 us
    dot_general x30, matrix products, right_product(): lax.dot_general(left, right, (((1,), (1,)), ((), ())), preferred_element_...  57.2 us
    psum x1, waiting for transfers between devices, per_device(): delta = lax.psum(anchor - new_inner, 'grp') / lax.axis_size('grp')  37.8 us
    reduce_sum x2, other arithmetic, vocab_head(): target_logit = jnp.sum(jnp.where(hit, logits, 0.0), axis=1)  32.5 us
    sub x6, matrix products, attend(): shifted = jnp.exp(scores - peak)  28.1 us
    dot_general x36, matrix products, left_product(): lax.dot_general(left, right, (((0,), (0,)), ((), ())), preferred_element_...  27.9 us
    psum x1, waiting for transfers between devices, per_device(): lax.psum((grad_total, loss_total, count_total), 'dp')  26.9 us
  transfers between devices with their start and end apart: 3, of which 3 were waited for; matrix products, arithmetic and copies ran while one was open for 9% of the time, Pallas kernels for 0%

commit v1 on v0

v1 whole, which is shorter than its diff:
```python
import functools

import jax
import jax.numpy as jnp
from jax import lax
from jax.experimental import pallas as pl
from jax.experimental.pallas import tpu as pltpu
from jax.sharding import PartitionSpec as P

D = 512
HEADS = 8
SIDE = 64
SIDE_HEADS = 8
SIDE_FF = 256
STEP = 5


norm_eps = 1e-06
negative = -1000000000.0
beta_first = 0.9
beta_second = 0.99
adam_eps = 1e-08
learn_rate = 0.03
decay_rate = 0.01
clip_norm = 0.01
outer_rate = 0.7
outer_beta = 0.9


def layout():
    return [
        ("down", (4, D, SIDE)),
        ("attn_in", (3, SIDE, 3 * SIDE)),
        ("attn_out", (3, SIDE, SIDE)),
        ("ffn_in", (2, SIDE, SIDE_FF)),
        ("ffn_out", (2, SIDE_FF, SIDE)),
        ("upsample", (SIDE, D)),
        ("small", (9, SIDE)),
    ]


def unpack(flat):
    parts = {}
    offset = 0
    for label, shape in layout():
        count = 1
        for extent in shape:
            count = count * extent
        parts[label] = flat[offset : offset + count].reshape(shape)
        offset = offset + count
    return parts


LOG2E = 1.4426950408889634
masked = -1e30

def dot(left, right):
    return jnp.dot(left, right, preferred_element_type=jnp.float32)

def dot_t(left, right):
    return lax.dot_general(left, right, (((1,), (1,)), ((), ())), preferred_element_type=jnp.float32)

def rms_rows(values, gain):
    return values * lax.rsqrt(jnp.mean(values * values, axis=1, keepdims=True) + norm_eps) * gain

def gelu(values):
    inner = values * (0.7978845608028654 + 0.035677408136300125 * (values * values))
    return (0.5 * values) * (1.0 + jnp.tanh(inner))

def lane_heads(query, keys, values, key_bias, causal_bias):
    lane = lax.broadcasted_iota(jnp.int32, (1, 128), 1)
    scale = 0.125 * LOG2E
    mixed = []
    for pair in range(4):
        span = slice(128 * pair, 128 * pair + 128)
        q_pair, k_pair, v_pair = query[:, span], keys[:, span], values[:, span]
        halves = []
        for side in range(2):
            own = (lane < 64) if side == 0 else (lane >= 64)
            spare = lane == (64 if side == 0 else 0)
            q_head = jnp.where(own, q_pair, spare.astype(jnp.bfloat16))
            k_head = jnp.where(own, k_pair, jnp.where(spare, key_bias, jnp.bfloat16(0)))
            scores = dot_t(q_head, k_head)
            if causal_bias is not None:
                scores = scores + causal_bias
            peak = jnp.max(scores, axis=1, keepdims=True)
            weight = jnp.exp2((scores - peak) * scale)
            total = jnp.sum(weight, axis=1, keepdims=True)
            halves.append(dot(weight.astype(jnp.bfloat16), v_pair) / total)
        mixed.append(jnp.where(lane < 64, halves[0], halves[1]).astype(jnp.bfloat16))
    return jnp.concatenate(mixed, axis=1)

def bias_column(count, valid):
    place = lax.broadcasted_iota(jnp.int32, (count, 1), 0)
    return jnp.where(place < valid, 0.0, masked).astype(jnp.bfloat16)

def frozen_ffn(state_ref, out_ref, gain, win_ref, wout_ref, finish):
    tokens = state_ref.shape[0]
    tile = 256
    def step(i, carry):
        at = pl.ds(i * tile, tile)
        state = state_ref[at]
        normed = rms_rows(state, gain).astype(jnp.bfloat16)
        total = state
        for start in range(0, win_ref.shape[1], 512):
            hidden = gelu(dot(normed, win_ref[:, start:start + 512])).astype(jnp.bfloat16)
            total = total + dot(hidden, wout_ref[start:start + 512])
        out_ref[at] = finish(total).astype(out_ref.dtype)
        return carry
    lax.fori_loop(0, tokens // tile, step, 0)

def fetch(pairs, sems):
    copies = [pltpu.make_async_copy(src, dst, sems.at[i]) for i, (src, dst) in enumerate(pairs)]
    for copy in copies:
        copy.start()
    return copies

def encoder_kernel(len_ref, x_ref, gains_ref, attn_hbm, win_hbm, wout_hbm, out_ref, attn_ref, win_ref, wout_ref, qkv_ref, state_ref, sems):
    first, second, third, fourth = fetch([(attn_hbm.at[0, :, :3 * D], attn_ref.at[:, :3 * D]), (attn_hbm.at[0, :, 3 * D:], attn_ref.at[:, 3 * D:]), (win_hbm.at[0], win_ref), (wout_hbm.at[0], wout_ref)], sems)
    tokens = x_ref.shape[0]
    x = x_ref[...].astype(jnp.float32)
    normed = rms_rows(x, gains_ref[0:1]).astype(jnp.bfloat16)
    first.wait()
    qkv_ref[...] = dot(normed, attn_ref[:, :3 * D]).astype(jnp.bfloat16)
    bias = bias_column(tokens, len_ref[0])
    second.wait()
    def step(i, carry):
        at = pl.ds(i * 256, 256)
        mixed = lane_heads(qkv_ref[at, :D], qkv_ref[:, D:2 * D], qkv_ref[:, 2 * D:], bias, None)
        state_ref[at] = x_ref[at].astype(jnp.float32) + dot(mixed, attn_ref[:, 3 * D:])
        return carry
    lax.fori_loop(0, tokens // 256, step, 0)
    third.wait()
    fourth.wait()
    frozen_ffn(state_ref, out_ref, gains_ref[1:2], win_ref, wout_ref, lambda v: rms_rows(v, gains_ref[2:3]))

def decoder_kernel(len_ref, x_ref, encoded_ref, gains_ref, attn_hbm, win_hbm, wout_hbm, out_ref, attn_ref, cross_ref, win_ref, wout_ref, kv_ref, state_ref, sems):
    first, second, third, fourth = fetch([(attn_hbm.at[1], attn_ref), (attn_hbm.at[2], cross_ref), (win_hbm.at[1], win_ref), (wout_hbm.at[1], wout_ref)], sems)
    tokens = x_ref.shape[0]
    sources = encoded_ref.shape[0]
    x = x_ref[...].astype(jnp.float32)
    normed = rms_rows(x, gains_ref[3:4]).astype(jnp.bfloat16)
    row = lax.broadcasted_iota(jnp.int32, (tokens, tokens), 0)
    column = lax.broadcasted_iota(jnp.int32, (tokens, tokens), 1)
    causal = jnp.where(column <= row, 0.0, masked)
    first.wait()
    qkv = dot(normed, attn_ref[:, :3 * D]).astype(jnp.bfloat16)
    mixed = lane_heads(qkv[:, :D], qkv[:, D:2 * D], qkv[:, 2 * D:], bias_column(tokens, len_ref[1]), causal)
    state = x + dot(mixed, attn_ref[:, 3 * D:])
    second.wait()
    kv_ref[...] = dot(encoded_ref[...], cross_ref[:, D:3 * D]).astype(jnp.bfloat16)
    normed = rms_rows(state, gains_ref[4:5]).astype(jnp.bfloat16)
    query = dot(normed, cross_ref[:, :D]).astype(jnp.bfloat16)
    mixed = lane_heads(query, kv_ref[:, :D], kv_ref[:, D:], bias_column(sources, len_ref[0]), None)
    state_ref[...] = state + dot(mixed, cross_ref[:, 3 * D:])
    third.wait()
    fourth.wait()
    frozen_ffn(state_ref, out_ref, gains_ref[5:6], win_ref, wout_ref, lambda v: v)

smem = pl.BlockSpec(memory_space=pltpu.SMEM)
vmem = pl.BlockSpec(memory_space=pltpu.VMEM)
hbm = pl.BlockSpec(memory_space=pl.ANY)
LIMIT = pltpu.CompilerParams(vmem_limit_bytes=56 * 2**20)

def encode(lens, x, attn, ffn_in, ffn_out, gains):
    tokens = x.shape[0]
    return pl.pallas_call(
        encoder_kernel,
        out_shape=jax.ShapeDtypeStruct((tokens, D), jnp.bfloat16),
        in_specs=[smem, vmem, vmem, hbm, hbm, hbm],
        out_specs=vmem,
        scratch_shapes=[pltpu.VMEM((D, 4 * D), jnp.bfloat16), pltpu.VMEM((D, 4 * D), jnp.bfloat16), pltpu.VMEM((4 * D, D), jnp.bfloat16),
            pltpu.VMEM((tokens, 3 * D), jnp.bfloat16), pltpu.VMEM((tokens, D), jnp.float32), pltpu.SemaphoreType.DMA((4,))],
        compiler_params=LIMIT,
        name="encoder",
    )(lens, x, gains, attn, ffn_in, ffn_out)

def decode(lens, x, encoded, attn, ffn_in, ffn_out, gains):
    tokens = x.shape[0]
    sources = encoded.shape[0]
    return pl.pallas_call(
        decoder_kernel,
        out_shape=jax.ShapeDtypeStruct((tokens, D), jnp.bfloat16),
        in_specs=[smem, vmem, vmem, vmem, hbm, hbm, hbm],
        out_specs=vmem,
        scratch_shapes=[pltpu.VMEM((D, 4 * D), jnp.bfloat16), pltpu.VMEM((D, 4 * D), jnp.bfloat16), pltpu.VMEM((D, 4 * D), jnp.bfloat16), pltpu.VMEM((4 * D, D), jnp.bfloat16),
            pltpu.VMEM((sources, 2 * D), jnp.bfloat16), pltpu.VMEM((tokens, D), jnp.float32), pltpu.SemaphoreType.DMA((4,))],
        compiler_params=LIMIT,
        name="decoder",
    )(lens, x, encoded, gains, attn, ffn_in, ffn_out)

def dot_l(left, right):
    return lax.dot_general(left, right, (((0,), (0,)), ((), ())), preferred_element_type=jnp.float32)

def rms_columns(values, gain):
    return values * lax.rsqrt(jnp.mean(values * values, axis=0, keepdims=True) + norm_eps) * gain

def rms_columns_back(values, gain, grad):
    inverse = lax.rsqrt(jnp.mean(values * values, axis=0, keepdims=True) + norm_eps)
    gained = grad * gain
    along = jnp.mean(values * gained, axis=0, keepdims=True)
    gain_grad = jnp.sum(grad * (values * inverse), axis=1, keepdims=True)
    return inverse * gained - values * (inverse * inverse * inverse * along), gain_grad

def gelu_back(values, grad):
    square = values * values
    tanh = jnp.tanh(values * (0.7978845608028654 + 0.035677408136300125 * square))
    slope = 0.5 * (1.0 + tanh) + (0.5 * values) * (1.0 - tanh * tanh) * (0.7978845608028654 + 0.107032224408900375 * square)
    return grad * slope

side_scale = (SIDE // SIDE_HEADS) ** -0.5

def keys_with_bias(keys_t, valid):
    count = keys_t.shape[1]
    place = lax.broadcasted_iota(jnp.int32, (64, count), 1)
    line = lax.broadcasted_iota(jnp.int32, (64, count), 0)
    bias = jnp.where((line == 0) & (place >= valid), masked, 0.0)
    return jnp.concatenate([keys_t.astype(jnp.float32), bias], axis=0).T.astype(jnp.bfloat16)

def head_query(query_t, head):
    line = lax.broadcasted_iota(jnp.int32, (64, 1), 0)
    own = jnp.where(line // 8 == head, query_t, 0.0)
    ones = jnp.broadcast_to(jnp.where(line == 0, 1.0, 0.0), own.shape)
    return jnp.concatenate([own, ones], axis=0).astype(jnp.bfloat16)

def rounded(values):
    return values.astype(jnp.bfloat16).astype(jnp.float32)

def causal_columns(count):
    key = lax.broadcasted_iota(jnp.int32, (count, count), 0)
    query = lax.broadcasted_iota(jnp.int32, (count, count), 1)
    return jnp.where(key <= query, 0.0, masked)

def side_heads(query_t, keys_t, values_t, valid, causal):
    keys = keys_with_bias(keys_t, valid)
    outs, sums = [], []
    for head in range(SIDE_HEADS):
        scores = dot(keys, head_query(query_t, head))
        if causal is not None:
            scores = scores + causal
        peak = jnp.max(scores, axis=0, keepdims=True)
        weight = jnp.exp2((scores - peak) * (side_scale * LOG2E))
        total = jnp.sum(weight, axis=0, keepdims=True)
        span = slice(8 * head, 8 * head + 8)
        outs.append(dot(values_t[span].astype(jnp.bfloat16), weight.astype(jnp.bfloat16)) / total)
        sums.append(peak * (side_scale * LOG2E) + jnp.log2(total))
    return jnp.concatenate(outs, axis=0), jnp.concatenate(sums, axis=0)

def side_heads_back(query_t, keys_t, values_t, sums, grad_t, valid, causal):
    keys = keys_with_bias(keys_t, valid)
    values = values_t.T.astype(jnp.bfloat16)
    line = lax.broadcasted_iota(jnp.int32, (64, 1), 0)
    grad_q, grad_k, grad_v = [], [], []
    for head in range(SIDE_HEADS):
        span = slice(8 * head, 8 * head + 8)
        scores = dot(keys, head_query(query_t, head))
        if causal is not None:
            scores = scores + causal
        weight = jnp.exp2(scores * (side_scale * LOG2E) - sums[head:head + 1])
        own_grad = jnp.where(line // 8 == head, grad_t, 0.0).astype(jnp.bfloat16)
        grad_w = rounded(dot(values, own_grad))
        along = jnp.sum(grad_w * weight, axis=0, keepdims=True)
        grad_s = (weight * (grad_w - along)).astype(jnp.bfloat16)
        grad_q.append(dot(keys_t[span].astype(jnp.bfloat16), grad_s))
        grad_k.append(dot_t(query_t[span].astype(jnp.bfloat16), grad_s))
        grad_v.append(dot_t(grad_t[span].astype(jnp.bfloat16), weight.astype(jnp.bfloat16)))
    return (jnp.concatenate(grad_q, axis=0) * side_scale, jnp.concatenate(grad_k, axis=0) * side_scale,
            jnp.concatenate(grad_v, axis=0))

def chosen_columns(tokens, positions_ref):
    token = lax.broadcasted_iota(jnp.int32, (tokens, positions_ref.shape[1]), 0)
    return jnp.where(token == positions_ref[...], 1.0, 0.0).astype(jnp.bfloat16)

def side_kernel(len_ref, src_ref, encoded_ref, tgt_ref, decoded_ref, positions_ref, down_ref, attn_in_ref, attn_out_ref, ffn_in_ref, ffn_out_ref, small_ref,
                picked_ref, enc_ref, dec_ref, enc_mixed_ref, self_mixed_ref, cross_mixed_ref, enc_sums_ref, self_sums_ref, cross_sums_ref):
    def gain(i):
        return small_ref[:, i:i + 1]

    def attend(which, query_n, key_n, valid, causal, mixed_ref, sums_ref):
        query = rounded(dot(attn_in_ref[which, :64], query_n))
        keyval = rounded(dot(attn_in_ref[which, 64:], key_n))
        mixed, sums = side_heads(query, keyval[:64], keyval[64:], valid, causal)
        mixed_b = mixed.astype(jnp.bfloat16)
        mixed_ref[...] = mixed_b
        sums_ref[...] = sums
        return dot(attn_out_ref[which], mixed_b)

    def ffn(which, normed):
        active = gelu(dot(ffn_in_ref[which], normed)).astype(jnp.bfloat16)
        return dot(ffn_out_ref[which], active)

    def norm(values, i):
        return rms_columns(values, gain(i)).astype(jnp.bfloat16)

    source_valid, target_valid = len_ref[0], len_ref[1]
    state = dot_t(down_ref[0], src_ref[...])
    enc_ref[0] = state
    normed = norm(state, 0)
    state = state + attend(0, normed, normed, source_valid, None, enc_mixed_ref, enc_sums_ref)
    enc_ref[1] = state
    state = state + ffn(0, norm(state, 1))
    enc_ref[2] = state
    joined = dot_t(down_ref[1], encoded_ref[...])
    enc_ref[3] = joined
    gate = jax.nn.sigmoid(gain(7))
    memory = norm(gate * joined + (1.0 - gate) * state, 2)
    flow = dot_t(down_ref[2], tgt_ref[...])
    dec_ref[0] = flow
    normed = norm(flow, 3)
    causal = causal_columns(flow.shape[1])
    flow = flow + attend(1, normed, normed, target_valid, causal, self_mixed_ref, self_sums_ref)
    dec_ref[1] = flow
    flow = flow + attend(2, norm(flow, 4), memory, source_valid, None, cross_mixed_ref, cross_sums_ref)
    dec_ref[2] = flow
    flow = flow + ffn(1, norm(flow, 5))
    dec_ref[3] = flow
    joined = dot_t(down_ref[3], decoded_ref[...])
    dec_ref[4] = joined
    gate = jax.nn.sigmoid(gain(8))
    top = norm(gate * joined + (1.0 - gate) * flow, 6)
    picked = dot(top, chosen_columns(flow.shape[1], positions_ref)).astype(jnp.bfloat16)
    picked_ref[...] = picked

def side(lens, src, encoded, tgt, decoded, positions, weights):
    s, t, p = src.shape[0], tgt.shape[0], positions.shape[1]
    f32, bf16 = jnp.float32, jnp.bfloat16
    shapes = [((64, p), bf16), ((4, 64, s), f32), ((5, 64, t), f32), ((64, s), bf16), ((64, t), bf16), ((64, t), bf16), ((8, s), f32), ((8, t), f32), ((8, t), f32)]
    return pl.pallas_call(
        side_kernel,
        out_shape=[jax.ShapeDtypeStruct(*item) for item in shapes],
        in_specs=[smem] + [vmem] * 11,
        out_specs=[vmem] * 9,
        compiler_params=LIMIT,
        name="side",
    )(lens, src, encoded, tgt, decoded, positions, *weights)

def back_kernel(*refs, started):
    (len_ref, src_ref, encoded_ref, tgt_ref, decoded_ref, positions_ref, attn_in_t_ref, ffn_in_t_ref, attn_in_ref, attn_out_ref, ffn_in_ref, ffn_out_ref, small_ref,
     enc_ref, dec_ref, enc_mixed_ref, self_mixed_ref, cross_mixed_ref, enc_sums_ref, self_sums_ref, cross_sums_ref, parts_ref) = refs[:22]
    before = refs[22:28] if started else (None,) * 6
    down_out, attn_in_out, attn_out_out, ffn_in_out, ffn_out_out, small_out = refs[-6:]

    def put(which, index, values):
        refs_of = {"down": 0, "attn_in": 1, "attn_out": 2, "ffn_in": 3, "ffn_out": 4}
        at = refs_of[which]
        out = (down_out, attn_in_out, attn_out_out, ffn_in_out, ffn_out_out)[at]
        out[index] = values if before[at] is None else before[at][index] + values

    smalls = {}

    def gain(i):
        return small_ref[:, i:i + 1]

    def norm(values, i):
        return rms_columns(values, gain(i)).astype(jnp.bfloat16)

    def norm_back(values, i, grad):
        result, smalls[i] = rms_columns_back(values, gain(i), grad)
        return result

    def blend_back(i, joined, late, grad):
        gate = jax.nn.sigmoid(gain(i))
        smalls[i] = jnp.sum(grad * (joined - late), axis=1, keepdims=True) * (gate * (1.0 - gate))
        return gate * grad, (1.0 - gate) * grad

    def ffn_back(which, normed, grad):
        grad_b = grad.astype(jnp.bfloat16)
        hidden = dot(ffn_in_t_ref[which], normed)
        active = gelu(hidden).astype(jnp.bfloat16)
        put("ffn_out", which, dot_t(active, grad_b))
        grad_hidden = gelu_back(hidden, dot(ffn_out_ref[which], grad_b)).astype(jnp.bfloat16)
        put("ffn_in", which, dot_t(normed, grad_hidden))
        return dot(ffn_in_ref[which], grad_hidden)

    def attend_back(which, query_n, key_n, mixed_ref, sums_ref, grad, valid, causal):
        grad_b = grad.astype(jnp.bfloat16)
        put("attn_out", which, dot_t(mixed_ref[...], grad_b))
        grad_mixed = rounded(dot(attn_out_ref[which], grad_b))
        query = rounded(dot(attn_in_t_ref[which, :64], query_n))
        keyval = rounded(dot(attn_in_t_ref[which, 64:], key_n))
        grad_q, grad_k, grad_v = side_heads_back(query, keyval[:64], keyval[64:], sums_ref, grad_mixed, valid, causal)
        return grad_q.astype(jnp.bfloat16), jnp.concatenate([grad_k, grad_v], axis=0).astype(jnp.bfloat16)

    source_valid, target_valid = len_ref[0], len_ref[1]
    tokens = tgt_ref.shape[0]
    grad_picked = parts_ref[0].astype(jnp.float32)
    for i in range(1, parts_ref.shape[0]):
        grad_picked = grad_picked + parts_ref[i].astype(jnp.float32)
    chosen = chosen_columns(tokens, positions_ref)
    high = grad_picked.astype(jnp.bfloat16)
    low = (grad_picked - high.astype(jnp.float32)).astype(jnp.bfloat16)
    grad = dot_t(high, chosen) + dot_t(low, chosen)
    gate = jax.nn.sigmoid(gain(8))
    final = gate * dec_ref[4] + (1.0 - gate) * dec_ref[3]
    grad = norm_back(final, 6, grad)
    grad_joined, grad = blend_back(8, dec_ref[4], dec_ref[3], grad)
    put("down", 3, dot(grad_joined.astype(jnp.bfloat16), decoded_ref[...]))
    grad = grad + norm_back(dec_ref[2], 5, ffn_back(1, norm(dec_ref[2], 5), grad))
    gate = jax.nn.sigmoid(gain(7))
    final = gate * enc_ref[3] + (1.0 - gate) * enc_ref[2]
    memory = norm(final, 2)
    normed = norm(dec_ref[1], 4)
    grad_q, grad_kv = attend_back(2, normed, memory, cross_mixed_ref, cross_sums_ref, grad, source_valid, None)
    zero_q = jnp.zeros((128, tokens), jnp.bfloat16)
    zero_kv = jnp.zeros((64, src_ref.shape[0]), jnp.bfloat16)
    put("attn_in", 2, dot_t(normed, jnp.concatenate([grad_q, zero_q], axis=0)) + dot_t(memory, jnp.concatenate([zero_kv, grad_kv], axis=0)))
    weight = attn_in_ref[2]
    grad_memory = dot(weight, jnp.concatenate([zero_kv, grad_kv], axis=0))
    grad = grad + norm_back(dec_ref[1], 4, dot(weight, jnp.concatenate([grad_q, zero_q], axis=0)))
    normed = norm(dec_ref[0], 3)
    grad_q, grad_kv = attend_back(1, normed, normed, self_mixed_ref, self_sums_ref, grad, target_valid, causal_columns(tokens))
    grad_qkv = jnp.concatenate([grad_q, grad_kv], axis=0)
    put("attn_in", 1, dot_t(normed, grad_qkv))
    grad = grad + norm_back(dec_ref[0], 3, dot(attn_in_ref[1], grad_qkv))
    put("down", 2, dot(grad.astype(jnp.bfloat16), tgt_ref[...]))
    grad = norm_back(final, 2, grad_memory)
    grad_joined, grad = blend_back(7, enc_ref[3], enc_ref[2], grad)
    put("down", 1, dot(grad_joined.astype(jnp.bfloat16), encoded_ref[...]))
    grad = grad + norm_back(enc_ref[1], 1, ffn_back(0, norm(enc_ref[1], 1), grad))
    normed = norm(enc_ref[0], 0)
    grad_q, grad_kv = attend_back(0, normed, normed, enc_mixed_ref, enc_sums_ref, grad, source_valid, None)
    grad_qkv = jnp.concatenate([grad_q, grad_kv], axis=0)
    put("attn_in", 0, dot_t(normed, grad_qkv))
    grad = grad + norm_back(enc_ref[0], 0, dot(attn_in_ref[0], grad_qkv))
    put("down", 0, dot(grad.astype(jnp.bfloat16), src_ref[...]))
    lane = lax.broadcasted_iota(jnp.int32, (1, 128), 1)
    total = jnp.zeros((64, 128), jnp.float32) if before[5] is None else before[5][...]
    for i in range(9):
        total = total + jnp.where(lane == i, smalls[i], 0.0)
    small_out[...] = total

def side_back(lens, src, encoded, tgt, decoded, positions, weights, kept, parts, before):
    f32 = jnp.float32
    shapes = [(4, 64, 512), (3, 64, 192), (3, 64, 64), (2, 64, 256), (2, 256, 64), (64, 128)]
    extra = list(before) if before is not None else []
    return pl.pallas_call(
        functools.partial(back_kernel, started=before is not None),
        out_shape=[jax.ShapeDtypeStruct(shape, f32) for shape in shapes],
        in_specs=[smem] + [vmem] * (21 + len(extra)),
        out_specs=[vmem] * 6,
        compiler_params=LIMIT,
        name="side_back",
    )(lens, src, encoded, tgt, decoded, positions, *weights, *kept, parts, *extra)


def swap(values, axis, distance):
    size = lax.axis_size(axis)
    return lax.ppermute(values, axis, [(i, i ^ distance) for i in range(size)])


def gather_peers(values, axis):
    return [values] + [swap(values, axis, s) for s in range(1, lax.axis_size(axis))]


def exchange(pieces, axis):
    return [pieces[0]] + [swap(pieces[s], axis, s) for s in range(1, lax.axis_size(axis))]


def tree_sum(terms):
    while len(terms) > 1:
        terms = [terms[i] + terms[i + 1] for i in range(0, len(terms), 2)]
    return terms[0]


def round_bf16(values):
    return lax.reduce_precision(values, 8, 7)


def split_bf16(values):
    high = round_bf16(values)
    return high.astype(jnp.bfloat16), (values - high).astype(jnp.bfloat16)


def embed_rows(ids, table, rows):
    size = lax.axis_size("dp")
    count = ids.shape[0]
    me = lax.axis_index("dp")
    cap = -(-(count * 5 // (size * 6)) // 32) * 32
    total = size * cap
    place = jnp.arange(count)
    same = ids[:, None] == ids[None, :]
    first_at = jnp.min(jnp.where(same, place[None, :], count), axis=1)
    first = first_at == place
    owner = (ids // rows) ^ me
    ahead = (
        first[None, :] & (owner[None, :] == owner[:, None]) & (place[None, :] < first_at[:, None])
    )
    rank = jnp.sum(ahead.astype(jnp.int32), axis=1)
    local = ids % rows
    busiest = jnp.max(jnp.where(first, rank, 0)) + 1
    slot_owner = jnp.arange(total) // cap
    slot_rank = jnp.arange(total) % cap

    def one_round(start):
        hit = (
            first[None, :]
            & (owner[None, :] == slot_owner[:, None])
            & (rank[None, :] == slot_rank[:, None] + start)
        )
        wanted = jnp.sum(jnp.where(hit, local[None, :], 0), axis=1).reshape(size, cap)
        asked = jnp.stack(exchange([wanted[s] for s in range(size)], "dp"))
        found = jnp.take(table, asked.reshape(-1), axis=0, mode="clip").reshape(size, cap, -1)
        came = jnp.concatenate(exchange([found[s] for s in range(size)], "dp"))
        mine = (owner * cap + rank - start)[:, None] == jnp.arange(total)[None, :]
        mine = mine & (rank >= start)[:, None] & (rank < start + cap)[:, None]
        return jnp.dot(
            mine.astype(jnp.bfloat16), came, preferred_element_type=jnp.bfloat16
        )

    most = jnp.full((8, 128), busiest, jnp.int32)
    for axis in ("dp", "grp"):
        peers = gather_peers(most, axis)
        for peer in peers:
            most = jnp.maximum(most, peer)
    most = most[0, 0]
    result = one_round(0)
    return lax.while_loop(
        lambda carry: carry[0] < most,
        lambda carry: (carry[0] + cap, carry[1] + one_round(carry[0])),
        (jnp.int32(cap), result),
    )[1]


CHUNK = 512
TILE = 256


def stats_kernel(rows, weight_ref, picked_ref, target_ref, out_ref):
    picked = picked_ref[...]
    target = target_ref[...]
    peak = jnp.full((1, TILE), -jnp.inf, jnp.float32)
    total = jnp.zeros((1, TILE), jnp.float32)
    aim = jnp.zeros((1, TILE), jnp.float32)
    padded = weight_ref.shape[0]
    chunk = min(CHUNK, padded)
    for start in range(0, padded, chunk):
        logits = jnp.dot(
            weight_ref[start : start + chunk], picked, preferred_element_type=jnp.float32
        )
        place = lax.broadcasted_iota(jnp.int32, (chunk, TILE), 0) + start
        aim = aim + jnp.sum(jnp.where(place == target, logits, 0.0), axis=0, keepdims=True)
        if start + chunk > rows:
            logits = jnp.where(place < rows, logits, -jnp.inf)
        above = jnp.maximum(peak, jnp.max(logits, axis=0, keepdims=True))
        total = total * jnp.exp(peak - above) + jnp.sum(
            jnp.exp(logits - above), axis=0, keepdims=True
        )
        peak = above
    out_ref[...] = jnp.concatenate([peak, total, aim, jnp.zeros((5, TILE), jnp.float32)], axis=0)


def head_stats(weight, picked, target, rows):
    padded = weight.shape[0]
    many = picked.shape[1]

    def kernel(*refs):
        stats_kernel(rows, *refs)

    return pl.pallas_call(
        kernel,
        out_shape=jax.ShapeDtypeStruct((8, many), jnp.float32),
        grid=(many // TILE,),
        in_specs=[
            pl.BlockSpec((padded, 128), lambda i: (0, 0)),
            pl.BlockSpec((128, TILE), lambda i: (0, i)),
            pl.BlockSpec((1, TILE), lambda i: (0, i)),
        ],
        out_specs=pl.BlockSpec((8, TILE), lambda i: (0, i)),
        compiler_params=pltpu.CompilerParams(vmem_limit_bytes=48 * 2**20),
    )(weight, picked, target)


def grad_kernel(
    rows, weight_ref, table_ref, up_ref, picked_ref, target_ref, lse_ref, mask_ref, top_ref, up_grad_ref
):
    picked = picked_ref[...]
    target = target_ref[...]
    lse = lse_ref[...]
    mask = mask_ref[...]
    padded = weight_ref.shape[0]
    chunk = min(CHUNK, padded)
    lifted = jnp.zeros((table_ref.shape[0], TILE), jnp.float32)
    for start in range(0, padded, chunk):
        logits = jnp.dot(
            weight_ref[start : start + chunk], picked, preferred_element_type=jnp.float32
        )
        place = lax.broadcasted_iota(jnp.int32, (chunk, TILE), 0) + start
        share = jnp.exp(logits - lse)
        grad = mask * jnp.where(place == target, share - 1.0, share)
        if start + chunk > rows:
            grad = jnp.where(place < rows, grad, 0.0)
        lifted = lifted + jnp.dot(
            table_ref[:, start : start + chunk],
            grad.astype(jnp.bfloat16),
            preferred_element_type=jnp.float32,
        )
    lifted_b = (lifted * D ** (-0.5)).astype(jnp.bfloat16)
    top_ref[...] = jnp.dot(up_ref[...], lifted_b, preferred_element_type=jnp.float32).astype(
        top_ref.dtype
    )

    @pl.when(pl.program_id(0) == 0)
    def _():
        up_grad_ref[...] = jnp.zeros_like(up_grad_ref)

    up_grad_ref[...] += dot_t(picked[: up_grad_ref.shape[0]], lifted_b)


def head_grad(weight, table_t, up_b, picked, target, lse, mask, rows):
    padded = weight.shape[0]
    many = picked.shape[1]
    width = table_t.shape[0]

    def kernel(*refs):
        grad_kernel(rows, *refs)

    row_spec = pl.BlockSpec((1, TILE), lambda i: (0, i))
    return pl.pallas_call(
        kernel,
        out_shape=(
            jax.ShapeDtypeStruct((SIDE, many), jnp.bfloat16),
            jax.ShapeDtypeStruct((SIDE, width), jnp.float32),
        ),
        grid=(many // TILE,),
        in_specs=[
            pl.BlockSpec((padded, 128), lambda i: (0, 0)),
            pl.BlockSpec((width, padded), lambda i: (0, 0)),
            pl.BlockSpec((SIDE, width), lambda i: (0, 0)),
            pl.BlockSpec((128, TILE), lambda i: (0, i)),
            row_spec,
            row_spec,
            row_spec,
        ],
        out_specs=(
            pl.BlockSpec((SIDE, TILE), lambda i: (0, i)),
            pl.BlockSpec((SIDE, width), lambda i: (0, 0)),
        ),
        compiler_params=pltpu.CompilerParams(vmem_limit_bytes=48 * 2**20),
    )(weight, table_t, up_b, picked, target, lse, mask)


def per_device(
    source_ids,
    target_inputs,
    lengths,
    positions,
    target_ids,
    target_mask,
    table,
    backbone_attn,
    backbone_ffn_in,
    backbone_ffn_out,
    backbone_gains,
    inner_weights,
    first_moment,
    second_moment,
    anchor,
    outer_momentum,
):
    micro = source_ids.shape[0]
    src_tokens = source_ids.shape[2]
    tgt_tokens = target_inputs.shape[2]
    size = lax.axis_size("dp")
    me = lax.axis_index("dp")
    core = me & 1
    rows = table.shape[0]
    padded = -(-rows // 512) * 512
    id_list = jnp.concatenate([source_ids.reshape(-1), target_inputs.reshape(-1)])
    embedded = embed_rows(id_list, table, rows)
    parts = unpack(inner_weights[0])
    up_b = parts["upsample"].astype(jnp.bfloat16)
    table_pad = jnp.pad(table, ((0, padded - rows), (0, 0)))
    table_t = table_pad.T
    lifted_table = dot_t(table_pad, up_b) * D ** (-0.5)
    weight = jnp.concatenate(split_bf16(lifted_table), axis=1)
    goals = jnp.concatenate([target_ids[:, 0], target_mask[:, 0]])
    goal_peers = jnp.stack(gather_peers(goals, "dp"), axis=1)
    all_targets = goal_peers[:micro].reshape(micro, 1, -1) - me * rows
    all_masks = goal_peers[micro:].reshape(micro, 1, -1).astype(jnp.float32)
    count_total = tree_sum(
        [jnp.sum(goal_peers[micro:, s].astype(jnp.float32)) for s in range(size)]
    )
    low = {label: values.astype(jnp.bfloat16) for label, values in parts.items()}
    turned = {label: jnp.swapaxes(low[label], -1, -2) for label in ("down", "attn_in", "attn_out", "ffn_in", "ffn_out")}
    small = jnp.pad(parts["small"].T, ((0, 0), (0, 128 - 9)))
    ahead = [turned["down"], turned["attn_in"], turned["attn_out"], turned["ffn_in"], turned["ffn_out"], small]
    behind = [turned["attn_in"], turned["ffn_in"], low["attn_in"], low["attn_out"], low["ffn_in"], low["ffn_out"], small]
    states = []
    for index in range(micro):
        embed_src = embedded[index * src_tokens : (index + 1) * src_tokens]
        base = micro * src_tokens + index * tgt_tokens
        embed_tgt = embedded[base : base + tgt_tokens]
        lens = lengths[index, 0]
        encoded = encode(lens, embed_src, backbone_attn, backbone_ffn_in, backbone_ffn_out, backbone_gains)
        decoded = decode(lens, embed_tgt, encoded, backbone_attn, backbone_ffn_in, backbone_ffn_out, backbone_gains)
        picked_t, *kept = side(lens, embed_src, encoded, embed_tgt, decoded, positions[index], ahead)
        picked_all = jnp.concatenate(gather_peers(picked_t, "dp"), axis=1)
        picked_all = jnp.concatenate([picked_all, picked_all], axis=0)
        states.append((lens, embed_src, encoded, embed_tgt, decoded, kept, picked_all))
    heads = []
    loss_total = jnp.zeros((), jnp.float32)
    for index in range(micro):
        stats = head_stats(weight, states[index][6], all_targets[index], rows)
        spots = stats.shape[1] // size
        peers = [
            jnp.concatenate(
                [peer[:, (j ^ s) * spots : ((j ^ s) + 1) * spots] for j in range(size)], axis=1
            )
            for s, peer in enumerate(gather_peers(stats[:3], "dp"))
        ]
        peak = peers[0][0]
        for peer in peers[1:]:
            peak = jnp.maximum(peak, peer[0])
        total = tree_sum([peer[1] * jnp.exp(peer[0] - peak) for peer in peers])
        aim = tree_sum([peer[2] for peer in peers])
        lse = peak + jnp.log(total)
        losses = (all_masks[index, 0] * (lse - aim)).reshape(size, -1)
        loss_total = loss_total + tree_sum([jnp.sum(losses[s]) for s in range(size)])
        heads.append(lse[None])
    grads, grad_up = None, 0.0
    for index in range(micro):
        lens, embed_src, encoded, embed_tgt, decoded, kept, picked_all = states[index]
        top_parts, up_part = head_grad(
            weight,
            table_t,
            up_b,
            picked_all,
            all_targets[index],
            heads[index],
            all_masks[index],
            rows,
        )
        grad_up = grad_up + up_part
        spots = top_parts.shape[1] // size
        back = jnp.stack(
            exchange([top_parts[:, s * spots : (s + 1) * spots] for s in range(size)], "dp")
        )
        grads = side_back(
            lens, embed_src, encoded, embed_tgt, decoded, positions[index], behind, kept, back, grads
        )
    pieces = [jnp.swapaxes(grads[0], 1, 2), *grads[1:5], grad_up, grads[5][:, :9].T]
    grad_total = jnp.concatenate([piece.reshape(-1) for piece in pieces])
    length = grad_total.shape[0]
    half = -(-length // 2048) * 1024
    wide = jnp.pad(grad_total, (0, 2 * half - length)).reshape(2, half)
    mine = lax.dynamic_index_in_dim(wide, core, 0, keepdims=False)
    other = lax.dynamic_index_in_dim(wide, 1 - core, 0, keepdims=False)
    mine = mine + swap(other, "dp", 1)
    sent = mine.astype(jnp.bfloat16)
    terms = [sent] + [swap(sent, "dp", s) for s in range(2, size, 2)]
    summed = tree_sum([term.astype(jnp.float32) for term in terms])
    both = swap(summed, "dp", 1)
    grad_total = jnp.where(core == 0, jnp.stack([summed, both]), jnp.stack([both, summed]))
    grad_total = grad_total.reshape(-1)[:length]
    mean_grad = grad_total / count_total
    norm = jnp.sqrt(jnp.sum(mean_grad * mean_grad))
    clipped = mean_grad * jnp.minimum(1.0, clip_norm / norm)
    moment_one = beta_first * first_moment[0] + (1.0 - beta_first) * clipped
    moment_two = beta_second * second_moment[0] + (1.0 - beta_second) * clipped * clipped
    fixed_one = moment_one / (1.0 - beta_first**STEP)
    fixed_two = moment_two / (1.0 - beta_second**STEP)
    old_weights = inner_weights[0]
    new_inner = old_weights - learn_rate * (
        fixed_one / (jnp.sqrt(fixed_two) + adam_eps) + decay_rate * old_weights
    )
    gap = jnp.pad(anchor - new_inner, (0, 2 * half - length)).reshape(2, half)
    sent = lax.dynamic_index_in_dim(gap, core, 0, keepdims=False).astype(jnp.bfloat16)
    terms = gather_peers(sent, "grp")
    summed = tree_sum([term.astype(jnp.float32) for term in terms]) / lax.axis_size("grp")
    both = swap(summed, "dp", 1)
    delta = jnp.where(core == 0, jnp.stack([summed, both]), jnp.stack([both, summed]))
    delta = delta.reshape(-1)[:length]
    momentum = outer_beta * outer_momentum + delta
    new_anchor = anchor - outer_rate * (delta + outer_beta * momentum)
    return (
        loss_total[None],
        count_total[None],
        norm[None],
        moment_one[None],
        moment_two[None],
        new_inner[None],
        delta,
        momentum,
        new_anchor,
    )


def solution(mesh):
    return jax.shard_map(
        per_device,
        mesh=mesh,
        in_specs=(
            P(None, ("grp", "dp"), None),
            P(None, ("grp", "dp"), None),
            P(None, ("grp", "dp"), None),
            P(None, ("grp", "dp"), None),
            P(None, ("grp", "dp"), None),
            P(None, ("grp", "dp"), None),
            P("dp", None),
            P(),
            P(),
            P(),
            P(),
            P("grp", None),
            P("grp", None),
            P("grp", None),
            P(),
            P(),
        ),
        out_specs=(
            P("grp"),
            P("grp"),
            P("grp"),
            P("grp", None),
            P("grp", None),
            P("grp", None),
            P(),
            P(),
            P(),
        ),
        check_vma=False,
    )
```

time: 828 us -> 552 us (0.67)
  matrix products: 270 us -> 6.75 us
  waiting for transfers between devices: 310 us -> 73.2 us
  Pallas kernels: 0 us -> 199 us
  starting transfers between devices: 0.12 us -> 106 us
  other arithmetic: 112 us -> 60.2 us
  local copies, waits for them, and re-layouts: 88.4 us -> 73.1 us
  blocking collectives: 13.6 us -> 0 us
    all_gather x1 -> x0, waiting for transfers between devices: 244 us -> none  [per_device(): table_rows = lax.all_gather(table, 'dp', axis=0, tiled=True)]
    dot_general x166 -> x2, matrix products: 242 us -> 6.75 us  [the longest x1 5.45 us: one_round(): jnp.dot(mine.astype(jnp.bfloat16), came, preferred_element_type=jnp.bfloa...]
    pallas_call x0 -> x12, Pallas kernels: none -> 199 us  [the longest x2 56.8 us: head_grad(): pl.pallas_call(kernel, out_shape=(jax.ShapeDtypeStruct((SIDE, many), jnp....]
    ppermute x0 -> x82, starting transfers between devices: none -> 106 us  [swap(): return lax.ppermute(values, axis, [(i, i ^ distance) for i in range(size)])]
    ppermute x0 -> x82, waiting for transfers between devices: none -> 73.2 us  [swap(): return lax.ppermute(values, axis, [(i, i ^ distance) for i in range(size)])]
    psum x2 -> x0, waiting for transfers between devices: 64.8 us -> none  [the longest x1 37.8 us: per_device(): delta = lax.psum(anchor - new_inner, 'grp') / lax.axis_size('grp')]
    reduce_sum x16 -> x12, other arithmetic: 42.5 us -> 12.2 us  [the longest x8 4.98 us: per_device(): jnp.sum(goal_peers[micro:, s].astype(jnp.float32))]
    sub x6 -> x0, matrix products: 28.1 us -> none  [attend(): shifted = jnp.exp(scores - peak)]
  transfers between devices with their start and end apart: 3 -> 82, of which waited for: 3 -> 22; matrix products, arithmetic and copies ran while one was open for 9% -> 17% of each run, Pallas kernels for 0% -> 26%
where the time goes in v1:
time: 552 us; the launch traced here: 542 us
  Pallas kernels  199 us (36%)
  starting transfers between devices  106 us (19%)
  waiting for transfers between devices  73.2 us (13%)
  local copies, waits for them, and re-layouts  73.1 us (13%)
  other arithmetic  60.2 us (11%)
  between operations  23.2 us (4%)
  matrix products  6.75 us (1%)
    ppermute x82, starting transfers between devices, swap(): return lax.ppermute(values, axis, [(i, i ^ distance) for i in range(size)])  106 us
    ppermute x82, waiting for transfers between devices, swap(): return lax.ppermute(values, axis, [(i, i ^ distance) for i in range(size)])  73.2 us
    pallas_call x2, Pallas kernels, head_grad(): pl.pallas_call(kernel, out_shape=(jax.ShapeDtypeStruct((SIDE, many), jnp....  56.8 us
    pallas_call x2, Pallas kernels, side_back(): pl.pallas_call(functools.partial(back_kernel, started=before is not None)...  39 us
    pallas_call x2, Pallas kernels, side(): pl.pallas_call(side_kernel, out_shape=[jax.ShapeDtypeStruct(*item) for it...  28.4 us
    pallas_call x2, Pallas kernels, encode(): pl.pallas_call(encoder_kernel, out_shape=jax.ShapeDtypeStruct((tokens, D)...  27.7 us
    pallas_call x2, Pallas kernels, head_stats(): pl.pallas_call(kernel, out_shape=jax.ShapeDtypeStruct((8, many), jnp.floa...  26.2 us
    pallas_call x2, Pallas kernels, decode(): pl.pallas_call(decoder_kernel, out_shape=jax.ShapeDtypeStruct((tokens, D)...  20.7 us
  transfers between devices with their start and end apart: 82, of which 22 were waited for; matrix products, arithmetic and copies ran while one was open for 17% of the time, Pallas kernels for 26%

profile of v1, /device:TPU:9, one launch (start us, length us, event | category | flops | bytes accessed | tf_op | source)
XLA Modules:
  0.0 541.5 jit_solution(16288098643591787467)
XLA Ops:
  16.2 12.3 %fusion.65 = (f32[279104]{0:T(1024)}, bf16[1,279104]{1,0:T(2,128)(2,1)S(1)}) fusion(f32[1,279104]{1,0:T(1,128)} %param.29), kind=kLoop, calls=%fused_computation.323 | loop fusion | flops 279104 | bytes 2791040 | tf_op args[11]
  39.4 6.7 %copy.73 = bf16[4016,512]{0,1:T(8,128)(2,1)} copy(bf16[4016,512]{1,0:T(8,128)(2,1)} %param.24) | data formatting | bytes 8224768 | tf_op args[6]
  46.1 4.9 pad_bitcast_fusion.refs_1_
  53.9 13.0 %multiply_reduce_fusion.1 = (f32[279104]{0:T(1024)}, f32[279104]{0:T(1024)}) fusion(f32[1,279104]{1,0:T(1,128)S(1)} %copy-done.9, f32[1,279104]{1,0:T(1,128)S(1)} %copy-done.10), kind=kLoop, calls=%fused_computation.67 | loop fusion | flops 558208 | bytes 4465664 | tf_op jit(solution)/shard_map/mul | solution.py:759
  73.5 3.7 collective-permute-start.38
  77.3 6.8 %gather_fusion.1 = bf16[1280,512]{1,0:T(8,128)(2,1)S(1)} fusion(bf16[4016,512]{1,0:T(8,128)(2,1)} %param.24, s32[2048]{0:T(1024)S(1)} %pad_clamp_fusion.1), kind=kCustom, calls=%fused_computation.1 | custom fusion | bytes 2626560 | tf_op jit(solution)/shard_map/jit(_take)/gather | solution.py:502
  89.8 3.7 collective-permute-start.17
  118.9 4.5 collective-permute-start.34
  124.8 12.4 %collective-permute-done.32 = bf16[160,512]{1,0:T(8,128)(2,1)S(1)} collective-permute-done((bf16[160,512]{1,0:T(8,128)(2,1)S(1)}, bf16[160,512]{1,0:T(8,128)(2,1)S(1)}, u32[]{:S(2)}, u32[]{:S(2)}) %collective-permute-start.32) | collective-permute-done | bytes 163872 | tf_op jit(solution)/shard_map/ppermute | solution.py:448
  144.9 5.4 %fusion.25 = bf16[1536,512]{1,0:T(8,128)(2,1)} fusion(bf16[1280,512]{1,0:T(8,128)(2,1)} %constant_dynamic-update-slice_fusion.15, s32[1536]{0:T(1024)S(1)} %copy-done.91, pred[1536]{0:T(1024)(128)(4,1)S(1)} %copy-done.97, pred[1536]{0:T(1024)(128)(4,1)S(1)} %copy-done.96), kind=kOutput, calls=%fused_computation.45 | convolution fusion | flops 2019164160 | bytes 2892800 | tf_op jit(solution)/shard_map/dot_general | solution.py:506
  155.1 14.0 %encoder.2.encoded_ref.refs_2_ = bf16[512,512]{1,0:T(8,128)(2,1)} custom-call(s32[2]{0:T(128)} %get-tuple-element.325.len_ref.refs_0_, bf16[512,512]{1,0:T(8,128)(2,1)} %get-tuple-element.232.x_ref.src_ref.refs_1_, f32[6,512]{1,0:T(8,128)} %gains_ref.7, bf16[3,512,2048]{2,1,0:T(8,128)(2,1)} %attn_hbm.7, bf16[2,512,2048]{2,1,0:T(8,128)(2,1)} %win_hbm.7, ...), custom_call_target="tpu_custom_call" | custom-call | tf_op jit(solution)/shard_map/encoder/pallas_call | solution.py:167
  169.0 10.3 %decoder.2.decoded_ref.refs_4_ = bf16[256,512]{1,0:T(8,128)(2,1)} custom-call(s32[2]{0:T(128)} %get-tuple-element.325.len_ref.refs_0_, bf16[256,512]{1,0:T(8,128)(2,1)} %get-tuple-element.230.x_ref.tgt_ref.refs_3_, bf16[512,512]{1,0:T(8,128)(2,1)} %encoder.2.encoded_ref.refs_2_, f32[6,512]{1,0:T(8,128)} %gains_ref.7, bf16[3,512,2048]{2,1,0:T(8,128)(2,1)} %attn_hbm.7, ...), custom_call_target="tpu_custom_call" | custom-call | tf_op jit(solution)/shard_map/decoder/pallas_call | solution.py:181
  179.4 14.3 %side.2 = (bf16[64,256]{1,0:T(8,128)(2,1)}, f32[4,64,512]{2,1,0:T(8,128)}, f32[5,64,256]{2,1,0:T(8,128)}, bf16[64,512]{1,0:T(8,128)(2,1)}, bf16[64,256]{1,0:T(8,...) custom-call(s32[2]{0:T(128)} %get-tuple-element.325.len_ref.refs_0_, ...), custom_call_target="tpu_custom_call" | custom-call | tf_op jit(solution)/shard_map/side/pallas_call | solution.py:328
  197.2 13.8 %encoder.3.encoded_ref.refs_2_ = bf16[512,512]{1,0:T(8,128)(2,1)} custom-call(s32[2]{0:T(128)} %get-tuple-element.324.len_ref.refs_0_, bf16[512,512]{1,0:T(8,128)(2,1)} %get-tuple-element.231.x_ref.src_ref.refs_1_, f32[6,512]{1,0:T(8,128)} %gains_ref.7, bf16[3,512,2048]{2,1,0:T(8,128)(2,1)} %attn_hbm.7, bf16[2,512,2048]{2,1,0:T(8,128)(2,1)} %win_hbm.7, ...), custom_call_target="tpu_custom_call" | custom-call | tf_op jit(solution)/shard_map/encoder/pallas_call | solution.py:167
  210.9 10.4 %decoder.3.decoded_ref.refs_4_ = bf16[256,512]{1,0:T(8,128)(2,1)} custom-call(s32[2]{0:T(128)} %get-tuple-element.324.len_ref.refs_0_, bf16[256,512]{1,0:T(8,128)(2,1)} %get-tuple-element.229.x_ref.tgt_ref.refs_3_, bf16[512,512]{1,0:T(8,128)(2,1)} %encoder.3.encoded_ref.refs_2_, f32[6,512]{1,0:T(8,128)} %gains_ref.7, bf16[3,512,2048]{2,1,0:T(8,128)(2,1)} %attn_hbm.7, ...), custom_call_target="tpu_custom_call" | custom-call | tf_op jit(solution)/shard_map/decoder/pallas_call | solution.py:181
  221.4 14.1 %side.3 = (bf16[64,256]{1,0:T(8,128)(2,1)}, f32[4,64,512]{2,1,0:T(8,128)}, f32[5,64,256]{2,1,0:T(8,128)}, bf16[64,512]{1,0:T(8,128)(2,1)}, bf16[64,256]{1,0:T(8,...) custom-call(s32[2]{0:T(128)} %get-tuple-element.324.len_ref.refs_0_, ...), custom_call_target="tpu_custom_call" | custom-call | tf_op jit(solution)/shard_map/side/pallas_call | solution.py:328
  261.2 6.8 %collective-permute-start.49 = (bf16[64,256]{1,0:T(8,128)(2,1)S(1)}, bf16[64,256]{1,0:T(8,128)(2,1)S(1)}, u32[]{:S(2)}, u32[]{:S(2)}) collective-permute-start(bf16[64,256]{1,0:T(8,128)(2,1)S(1)} %copy-done.73), channel_id=1, source_target_pairs={{0,5},{1,4},{2,7},{3,6},{4,1},{5,0},{6,3},{7,2},{8,13},{9,12},{10,... | collective-permute-start | bytes 98312 | tf_op jit(solution)/shard_map/ppermute | solution.py:448
  268.9 13.1 %shard_map.224 = f32[8,2048]{1,0:T(8,128)S(1)} custom-call(bf16[4096,128]{1,0:T(8,128)(2,1)S(1)} %pad_maximum_fusion.refs_0_, bf16[128,2048]{1,0:T(8,128)(2,1)S(1)} %pad_maximum_fusion.2.refs_1_.refs_3_, s32[1,2048]{1,0:T(1,128)S(1)} %bitcast.173), custom_call_target="tpu_custom_call" | custom-call | tf_op jit(solution)/shard_map/pallas_call | solution.py:559
  283.0 13.1 %shard_map.223 = f32[8,2048]{1,0:T(8,128)S(1)} custom-call(bf16[4096,128]{1,0:T(8,128)(2,1)S(1)} %pad_maximum_fusion.refs_0_, bf16[128,2048]{1,0:T(8,128)(2,1)S(1)} %pad_maximum_fusion.1.refs_1_.refs_3_, s32[1,2048]{1,0:T(1,128)S(1)} %bitcast.175), custom_call_target="tpu_custom_call" | custom-call | tf_op jit(solution)/shard_map/pallas_call | solution.py:559
  312.4 28.2 %shard_map.226 = (bf16[64,2048]{1,0:T(8,128)(2,1)S(1)}, f32[64,512]{1,0:T(8,128)S(1)}) custom-call(bf16[4096,128]{1,0:T(8,128)(2,1)S(1)} %pad_maximum_fusion.refs_0_, bf16[512,4096]{1,0:T(8,128)(2,1)} %pad_bitcast_fusion.refs_1_, bf16[64,512]{1,0:T(8,128)(2,1)S(1)} %convert_element_type.107.refs_2_, bf16[128,2048]{1,0:T(8,128)(2,1)S(1)} %pad_maximum_fusion.1.refs_1_.refs_3_, ...), custom_call_target="tpu_custom_call" | custom-call | tf_op jit(solution)/shard_map/pallas_call | solution.py:618
  344.3 28.6 %shard_map.225 = (bf16[64,2048]{1,0:T(8,128)(2,1)S(1)}, f32[64,512]{1,0:T(8,128)S(1)}) custom-call(bf16[4096,128]{1,0:T(8,128)(2,1)S(1)} %pad_maximum_fusion.refs_0_, bf16[512,4096]{1,0:T(8,128)(2,1)} %pad_bitcast_fusion.refs_1_, bf16[64,512]{1,0:T(8,128)(2,1)S(1)} %convert_element_type.107.refs_2_, bf16[128,2048]{1,0:T(8,128)(2,1)S(1)} %pad_maximum_fusion.2.refs_1_.refs_3_, ...), custom_call_target="tpu_custom_call" | custom-call | tf_op jit(solution)/shard_map/pallas_call | solution.py:618
  393.4 19.3 %side_back.2 = (f32[4,64,512]{2,1,0:T(8,128)}, f32[3,64,192]{2,1,0:T(8,128)}, f32[3,64,64]{2,1,0:T(8,128)}, f32[2,64,256]{2,1,0:T(8,128)}, f32[2,256,64]{2,1,0:T(8,128)}, /*index=5*/f32[64,128]{1,0:T(8,128)}) custom-call(s32[2]{0:T(128)} %get-tuple-element.325.len_ref.refs_0_, bf16[512,512]{1,0:T(8,128)(2,1)} %get-tuple-element.232.x_ref.src_ref.refs_1_, ...), custom_call_target="tpu_custom_call" | custom-call | tf_op jit(solution)/shard_map/side_back/pallas_call | solution.py:436
  413.4 19.7 %side_back.3 = (f32[4,64,512]{2,1,0:T(8,128)}, f32[3,64,192]{2,1,0:T(8,128)}, f32[3,64,64]{2,1,0:T(8,128)}, f32[2,64,256]{2,1,0:T(8,128)}, f32[2,256,64]{2,1,0:T(8,128)}, /*index=5*/f32[64,128]{1,0:T(8,128)}) custom-call(s32[2]{0:T(128)} %get-tuple-element.324.len_ref.refs_0_, bf16[512,512]{1,0:T(8,128)(2,1)} %get-tuple-element.231.x_ref.src_ref.refs_1_, ...), custom_call_target="tpu_custom_call" | custom-call | tf_op jit(solution)/shard_map/side_back/pallas_call | solution.py:436
  444.4 9.6 %collective-permute-done.88 = bf16[140288]{0:T(1024)(128)(2,1)S(1)} collective-permute-done((bf16[140288]{0:T(1024)(128)(2,1)S(1)}, bf16[140288]{0:T(1024)(128)(2,1)S(1)}, u32[]{:S(2)}, u32[]{:S(2)}) %collective-permute-start.88) | collective-permute-done | bytes 280608 | tf_op jit(solution)/shard_map/ppermute | solution.py:448
  456.4 12.5 %collective-permute-done.90 = bf16[140288]{0:T(1024)(128)(2,1)S(1)} collective-permute-done((bf16[140288]{0:T(1024)(128)(2,1)S(1)}, bf16[140288]{0:T(1024)(128)(2,1)S(1)}, u32[]{:S(2)}, u32[]{:S(2)}) %collective-permute-start.90) | collective-permute-done | bytes 280608 | tf_op jit(solution)/shard_map/ppermute | solution.py:448
  475.2 4.2 fusion.58
  479.8 4.1 convert_reduce_fusion.1
  486.7 5.2 collective-permute-done.92
  492.8 6.1 %collective-permute-done.94 = bf16[140288]{0:T(1024)(128)(2,1)S(1)} collective-permute-done((bf16[140288]{0:T(1024)(128)(2,1)S(1)}, bf16[140288]{0:T(1024)(128)(2,1)S(1)}, u32[]{:S(2)}, u32[]{:S(2)}) %collective-permute-start.94) | collective-permute-done | bytes 280608 | tf_op jit(solution)/shard_map/ppermute | solution.py:448
  513.1 6.1 %broadcast_in_dim.109 = f32[1,279104]{1,0:T(1,128)} reshape(f32[279104]{0:T(1024)} %get-tuple-element.192) | data formatting | bytes 2232832 | tf_op jit(solution)/shard_map/broadcast_in_dim | solution.py:779
  519.1 5.9 %broadcast_in_dim.110 = f32[1,279104]{1,0:T(1,128)} reshape(f32[279104]{0:T(1024)S(1)} %copy-done.3) | data formatting | bytes 2232832 | tf_op jit(solution)/shard_map/broadcast_in_dim | solution.py:780
  525.1 5.9 %broadcast_in_dim.111 = f32[1,279104]{1,0:T(1,128)} reshape(f32[279104]{0:T(1024)S(1)} %copy-done.2) | data formatting | bytes 2232832 | tf_op jit(solution)/shard_map/broadcast_in_dim | solution.py:781
  (566 shorter events, 179.4 us)
Async XLA Ops:
  10.9 57.8 %collective-permute-start.21 = (s32[160]{0:T(256)S(1)}, s32[160]{0:T(256)S(1)}, u32[]{:S(2)}, u32[]{:S(2)}) collective-permute-start(s32[160]{0:T(256)S(1)} %get-tuple-element.317), channel_id=1, source_target_pairs={{0,1},{1,0},{2,3},{3,2},{4,5},{5,4},{6,7},{7,6},{8,9},{9,8},{10,11... | collective-permute-start | bytes 1928 | tf_op jit(solution)/shard_map/ppermute | solution.py:448
  11.5 58.4 %collective-permute-start.22 = (s32[160]{0:T(256)S(1)}, s32[160]{0:T(256)S(1)}, u32[]{:S(2)}, u32[]{:S(2)}) collective-permute-start(s32[160]{0:T(256)S(1)} %get-tuple-element.316), channel_id=1, source_target_pairs={{0,2},{1,3},{2,0},{3,1},{4,6},{5,7},{6,4},{7,5},{8,10},{9,11},{10,... | collective-permute-start | bytes 1928 | tf_op jit(solution)/shard_map/ppermute | solution.py:448
  11.5 59.5 %collective-permute-start.23 = (s32[160]{0:T(256)S(1)}, s32[160]{0:T(256)S(1)}, u32[]{:S(2)}, u32[]{:S(2)}) collective-permute-start(s32[160]{0:T(256)S(1)} %get-tuple-element.315), channel_id=1, source_target_pairs={{0,3},{1,2},{2,1},{3,0},{4,7},{5,6},{6,5},{7,4},{8,11},{9,10},{10,... | collective-permute-start | bytes 1928 | tf_op jit(solution)/shard_map/ppermute | solution.py:448
  13.2 57.9 %collective-permute-start.24 = (s32[160]{0:T(256)S(1)}, s32[160]{0:T(256)S(1)}, u32[]{:S(2)}, u32[]{:S(2)}) collective-permute-start(s32[160]{0:T(256)S(1)} %get-tuple-element.314), channel_id=1, source_target_pairs={{0,4},{1,5},{2,6},{3,7},{4,0},{5,1},{6,2},{7,3},{8,12},{9,13},{10,... | collective-permute-start | bytes 1928 | tf_op jit(solution)/shard_map/ppermute | solution.py:448
  71.1 14.7 %collective-permute-start.36 = (s32[8,128]{1,0:T(8,128)S(1)}, s32[8,128]{1,0:T(8,128)S(1)}, u32[]{:S(2)}, u32[]{:S(2)}) collective-permute-start(s32[8,128]{1,0:T(8,128)S(1)} %broadcast_in_dim.105), channel_id=1, source_target_pairs={{0,2},{1,3},{2,0},{3,1},{4,6},{5,7},{6,4},{7,5},{8,10},{9,11},{10,... | collective-permute-start | bytes 12296 | tf_op jit(solution)/shard_map/ppermute | solution.py:448
  73.2 14.0 %collective-permute-start.37 = (s32[8,128]{1,0:T(8,128)S(1)}, s32[8,128]{1,0:T(8,128)S(1)}, u32[]{:S(2)}, u32[]{:S(2)}) collective-permute-start(s32[8,128]{1,0:T(8,128)S(1)} %broadcast_in_dim.105), channel_id=1, source_target_pairs={{0,3},{1,2},{2,1},{3,0},{4,7},{5,6},{6,5},{7,4},{8,11},{9,10},{10,... | collective-permute-start | bytes 12296 | tf_op jit(solution)/shard_map/ppermute | solution.py:448
  73.5 13.8 %collective-permute-start.38 = (s32[8,128]{1,0:T(8,128)S(1)}, s32[8,128]{1,0:T(8,128)S(1)}, u32[]{:S(2)}, u32[]{:S(2)}) collective-permute-start(s32[8,128]{1,0:T(8,128)S(1)} %broadcast_in_dim.105), channel_id=1, source_target_pairs={{0,4},{1,5},{2,6},{3,7},{4,0},{5,1},{6,2},{7,3},{8,12},{9,13},{10,... | collective-permute-start | bytes 12296 | tf_op jit(solution)/shard_map/ppermute | solution.py:448
  95.8 20.3 %collective-permute-start.28 = (bf16[160,512]{1,0:T(8,128)(2,1)}, bf16[160,512]{1,0:T(8,128)(2,1)S(1)}, u32[]{:S(2)}, u32[]{:S(2)}) collective-permute-start(bf16[160,512]{1,0:T(8,128)(2,1)} %get-tuple-element.239), channel_id=1, source_target_pairs={{0,1},{1,0},{2,3},{3,2},{4,5},{5,4},{6,7},{7,6},{8,9},{9,8},{10,11... | collective-permute-start | bytes 491528 | tf_op jit(solution)/shard_map/ppermute | solution.py:448
  95.8 16.1 %collective-permute-start.42 = (s32[8,128]{1,0:T(8,128)S(1)}, s32[8,128]{1,0:T(8,128)S(1)}, u32[]{:S(2)}, u32[]{:S(2)}) collective-permute-start(s32[8,128]{1,0:T(8,128)S(1)} %maximum_maximum_fusion.1), channel_id=1, source_target_pairs={{0,8},{8,0},{16,24},{24,16},{1,9},{9,1},{17,25},{25,17},{2,10},{10... | collective-permute-start | bytes 12296 | tf_op jit(solution)/shard_map/ppermute | solution.py:448
  97.6 14.7 %collective-permute-start.43 = (s32[8,128]{1,0:T(8,128)S(1)}, s32[8,128]{1,0:T(8,128)S(1)}, u32[]{:S(2)}, u32[]{:S(2)}) collective-permute-start(s32[8,128]{1,0:T(8,128)S(1)} %maximum_maximum_fusion.1), channel_id=1, source_target_pairs={{0,16},{8,24},{16,0},{24,8},{1,17},{9,25},{17,1},{25,9},{2,18},{10... | collective-permute-start | bytes 12296 | tf_op jit(solution)/shard_map/ppermute | solution.py:448
  98.8 16.7 %collective-permute-start.44 = (s32[8,128]{1,0:T(8,128)S(1)}, s32[8,128]{1,0:T(8,128)S(1)}, u32[]{:S(2)}, u32[]{:S(2)}) collective-permute-start(s32[8,128]{1,0:T(8,128)S(1)} %maximum_maximum_fusion.1), channel_id=1, source_target_pairs={{0,24},{8,16},{16,8},{24,0},{1,25},{9,17},{17,9},{25,1},{2,26},{10... | collective-permute-start | bytes 12296 | tf_op jit(solution)/shard_map/ppermute | solution.py:448
  116.0 21.1 %collective-permute-start.32 = (bf16[160,512]{1,0:T(8,128)(2,1)S(1)}, bf16[160,512]{1,0:T(8,128)(2,1)S(1)}, u32[]{:S(2)}, u32[]{:S(2)}) collective-permute-start(bf16[160,512]{1,0:T(8,128)(2,1)S(1)} %get-tuple-element.235), channel_id=1, source_target_pairs={{0,5},{1,4},{2,7},{3,6},{4,1},{5,0},{6,3},{7,2},{8,13},{9,12},{10,... | collective-permute-start | bytes 491528 | tf_op jit(solution)/shard_map/ppermute | solution.py:448
  116.7 24.1 %collective-permute-start.33 = (bf16[160,512]{1,0:T(8,128)(2,1)S(1)}, bf16[160,512]{1,0:T(8,128)(2,1)S(1)}, u32[]{:S(2)}, u32[]{:S(2)}) collective-permute-start(bf16[160,512]{1,0:T(8,128)(2,1)S(1)} %get-tuple-element.234), channel_id=1, source_target_pairs={{0,6},{1,7},{2,4},{3,5},{4,2},{5,3},{6,0},{7,1},{8,14},{9,15},{10,... | collective-permute-start | bytes 491528 | tf_op jit(solution)/shard_map/ppermute | solution.py:448
  118.9 25.4 %collective-permute-start.34 = (bf16[160,512]{1,0:T(8,128)(2,1)S(1)}, bf16[160,512]{1,0:T(8,128)(2,1)S(1)}, u32[]{:S(2)}, u32[]{:S(2)}) collective-permute-start(bf16[160,512]{1,0:T(8,128)(2,1)S(1)} %get-tuple-element.233), channel_id=1, source_target_pairs={{0,7},{1,6},{2,5},{3,4},{4,3},{5,2},{6,1},{7,0},{8,15},{9,14},{10,... | collective-permute-start | bytes 491528 | tf_op jit(solution)/shard_map/ppermute | solution.py:448
  194.4 73.7 %collective-permute-start.45 = (bf16[64,256]{1,0:T(8,128)(2,1)}, bf16[64,256]{1,0:T(8,128)(2,1)S(1)}, u32[]{:S(2)}, u32[]{:S(2)}) collective-permute-start(bf16[64,256]{1,0:T(8,128)(2,1)} %get-tuple-element.97), channel_id=1, source_target_pairs={{0,1},{1,0},{2,3},{3,2},{4,5},{5,4},{6,7},{7,6},{8,9},{9,8},{10,11... | collective-permute-start | bytes 98312 | tf_op jit(solution)/shard_map/ppermute | solution.py:448
  194.8 74.1 %collective-permute-start.46 = (bf16[64,256]{1,0:T(8,128)(2,1)}, bf16[64,256]{1,0:T(8,128)(2,1)S(1)}, u32[]{:S(2)}, u32[]{:S(2)}) collective-permute-start(bf16[64,256]{1,0:T(8,128)(2,1)} %get-tuple-element.97), channel_id=1, source_target_pairs={{0,2},{1,3},{2,0},{3,1},{4,6},{5,7},{6,4},{7,5},{8,10},{9,11},{10,... | collective-permute-start | bytes 98312 | tf_op jit(solution)/shard_map/ppermute | solution.py:448
  194.8 87.2 %collective-permute-start.47 = (bf16[64,256]{1,0:T(8,128)(2,1)}, bf16[64,256]{1,0:T(8,128)(2,1)S(1)}, u32[]{:S(2)}, u32[]{:S(2)}) collective-permute-start(bf16[64,256]{1,0:T(8,128)(2,1)} %get-tuple-element.97), channel_id=1, source_target_pairs={{0,3},{1,2},{2,1},{3,0},{4,7},{5,6},{6,5},{7,4},{8,11},{9,10},{10,... | collective-permute-start | bytes 98312 | tf_op jit(solution)/shard_map/ppermute | solution.py:448
  196.6 86.3 %collective-permute-start.48 = (bf16[64,256]{1,0:T(8,128)(2,1)}, bf16[64,256]{1,0:T(8,128)(2,1)S(1)}, u32[]{:S(2)}, u32[]{:S(2)}) collective-permute-start(bf16[64,256]{1,0:T(8,128)(2,1)} %get-tuple-element.97), channel_id=1, source_target_pairs={{0,4},{1,5},{2,6},{3,7},{4,0},{5,1},{6,2},{7,3},{8,12},{9,13},{10,... | collective-permute-start | bytes 98312 | tf_op jit(solution)/shard_map/ppermute | solution.py:448
  261.2 21.7 %collective-permute-start.49 = (bf16[64,256]{1,0:T(8,128)(2,1)S(1)}, bf16[64,256]{1,0:T(8,128)(2,1)S(1)}, u32[]{:S(2)}, u32[]{:S(2)}) collective-permute-start(bf16[64,256]{1,0:T(8,128)(2,1)S(1)} %copy-done.73), channel_id=1, source_target_pairs={{0,5},{1,4},{2,7},{3,6},{4,1},{5,0},{6,3},{7,2},{8,13},{9,12},{10,... | collective-permute-start | bytes 98312 | tf_op jit(solution)/shard_map/ppermute | solution.py:448
  268.1 14.8 %collective-permute-start.50 = (bf16[64,256]{1,0:T(8,128)(2,1)S(1)}, bf16[64,256]{1,0:T(8,128)(2,1)S(1)}, u32[]{:S(2)}, u32[]{:S(2)}) collective-permute-start(bf16[64,256]{1,0:T(8,128)(2,1)S(1)} %copy-done.73), channel_id=1, source_target_pairs={{0,6},{1,7},{2,4},{3,5},{4,2},{5,3},{6,0},{7,1},{8,14},{9,15},{10,... | collective-permute-start | bytes 98312 | tf_op jit(solution)/shard_map/ppermute | solution.py:448
  268.9 14.0 %collective-permute-start.51 = (bf16[64,256]{1,0:T(8,128)(2,1)S(1)}, bf16[64,256]{1,0:T(8,128)(2,1)S(1)}, u32[]{:S(2)}, u32[]{:S(2)}) collective-permute-start(bf16[64,256]{1,0:T(8,128)(2,1)S(1)} %copy-done.73), channel_id=1, source_target_pairs={{0,7},{1,6},{2,5},{3,4},{4,3},{5,2},{6,1},{7,0},{8,15},{9,14},{10,... | collective-permute-start | bytes 98312 | tf_op jit(solution)/shard_map/ppermute | solution.py:448
  282.1 19.0 %collective-permute-start.68 = (f32[3,2048]{1,0:T(4,128)S(1)}, f32[3,2048]{1,0:T(4,128)S(1)}, u32[]{:S(2)}, u32[]{:S(2)}) collective-permute-start(f32[3,2048]{1,0:T(4,128)S(1)} %slice.1225), channel_id=1, source_target_pairs={{0,3},{1,2},{2,1},{3,0},{4,7},{5,6},{6,5},{7,4},{8,11},{9,10},{10,... | collective-permute-start | bytes 73736 | tf_op jit(solution)/shard_map/ppermute | solution.py:448
  304.7 37.5 %collective-permute-start.66 = (f32[3,2048]{1,0:T(4,128)S(1)}, f32[3,2048]{1,0:T(4,128)S(1)}, u32[]{:S(2)}, u32[]{:S(2)}) collective-permute-start(f32[3,2048]{1,0:T(4,128)S(1)} %slice.1225), channel_id=1, source_target_pairs={{0,1},{1,0},{2,3},{3,2},{4,5},{5,4},{6,7},{7,6},{8,9},{9,8},{10,11... | collective-permute-start | bytes 73736 | tf_op jit(solution)/shard_map/ppermute | solution.py:448
  306.2 34.5 %collective-permute-start.70 = (f32[3,2048]{1,0:T(4,128)S(1)}, f32[3,2048]{1,0:T(4,128)S(1)}, u32[]{:S(2)}, u32[]{:S(2)}) collective-permute-start(f32[3,2048]{1,0:T(4,128)S(1)} %slice.1225), channel_id=1, source_target_pairs={{0,5},{1,4},{2,7},{3,6},{4,1},{5,0},{6,3},{7,2},{8,13},{9,12},{10,... | collective-permute-start | bytes 73736 | tf_op jit(solution)/shard_map/ppermute | solution.py:448
  308.2 35.0 %collective-permute-start.72 = (f32[3,2048]{1,0:T(4,128)S(1)}, f32[3,2048]{1,0:T(4,128)S(1)}, u32[]{:S(2)}, u32[]{:S(2)}) collective-permute-start(f32[3,2048]{1,0:T(4,128)S(1)} %slice.1225), channel_id=1, source_target_pairs={{0,7},{1,6},{2,5},{3,4},{4,3},{5,2},{6,1},{7,0},{8,15},{9,14},{10,... | collective-permute-start | bytes 73736 | tf_op jit(solution)/shard_map/ppermute | solution.py:448
  309.4 33.9 %collective-permute-start.67 = (f32[3,2048]{1,0:T(4,128)S(1)}, f32[3,2048]{1,0:T(4,128)S(1)}, u32[]{:S(2)}, u32[]{:S(2)}) collective-permute-start(f32[3,2048]{1,0:T(4,128)S(1)} %slice.1225), channel_id=1, source_target_pairs={{0,2},{1,3},{2,0},{3,1},{4,6},{5,7},{6,4},{7,5},{8,10},{9,11},{10,... | collective-permute-start | bytes 73736 | tf_op jit(solution)/shard_map/ppermute | solution.py:448
  310.3 33.0 %collective-permute-start.69 = (f32[3,2048]{1,0:T(4,128)S(1)}, f32[3,2048]{1,0:T(4,128)S(1)}, u32[]{:S(2)}, u32[]{:S(2)}) collective-permute-start(f32[3,2048]{1,0:T(4,128)S(1)} %slice.1225), channel_id=1, source_target_pairs={{0,4},{1,5},{2,6},{3,7},{4,0},{5,1},{6,2},{7,3},{8,12},{9,13},{10,... | collective-permute-start | bytes 73736 | tf_op jit(solution)/shard_map/ppermute | solution.py:448
  342.2 38.2 %collective-permute-start.80 = (bf16[64,256]{1,0:T(8,128)(2,1)S(1)}, bf16[64,256]{1,0:T(8,128)(2,1)S(1)}, u32[]{:S(2)}, u32[]{:S(2)}) collective-permute-start(bf16[64,256]{1,0:T(8,128)(2,1)S(1)} %get-tuple-element.251), channel_id=1, source_target_pairs={{0,1},{1,0},{2,3},{3,2},{4,5},{5,4},{6,7},{7,6},{8,9},{9,8},{10,11... | collective-permute-start | bytes 98312 | tf_op jit(solution)/shard_map/ppermute | solution.py:448
  390.3 22.4 %collective-permute-start.79 = (bf16[64,256]{1,0:T(8,128)(2,1)S(1)}, bf16[64,256]{1,0:T(8,128)(2,1)S(1)}, u32[]{:S(2)}, u32[]{:S(2)}) collective-permute-start(bf16[64,256]{1,0:T(8,128)(2,1)S(1)} %get-tuple-element.252), channel_id=1, source_target_pairs={{0,7},{1,6},{2,5},{3,4},{4,3},{5,2},{6,1},{7,0},{8,15},{9,14},{10,... | collective-permute-start | bytes 98312 | tf_op jit(solution)/shard_map/ppermute | solution.py:448
  440.6 13.4 %collective-permute-start.88 = (bf16[140288]{0:T(1024)(128)(2,1)S(1)}, bf16[140288]{0:T(1024)(128)(2,1)S(1)}, u32[]{:S(2)}, u32[]{:S(2)}) collective-permute-start(bf16[140288]{0:T(1024)(128)(2,1)S(1)} %add_convert_fusion), channel_id=1, source_target_pairs={{0,2},{1,3},{2,0},{3,1},{4,6},{5,7},{6,4},{7,5},{8,10},{9,11},{10,... | collective-permute-start | bytes 841736 | tf_op jit(solution)/shard_map/ppermute | solution.py:448
  443.6 25.2 %collective-permute-start.90 = (bf16[140288]{0:T(1024)(128)(2,1)S(1)}, bf16[140288]{0:T(1024)(128)(2,1)S(1)}, u32[]{:S(2)}, u32[]{:S(2)}) collective-permute-start(bf16[140288]{0:T(1024)(128)(2,1)S(1)} %add_convert_fusion), channel_id=1, source_target_pairs={{0,6},{1,7},{2,4},{3,5},{4,2},{5,3},{6,0},{7,1},{8,14},{9,15},{10,... | collective-permute-start | bytes 841736 | tf_op jit(solution)/shard_map/ppermute | solution.py:448
  499.9 31.1 %collective-permute-start.95 = (f32[140288]{0:T(1024)}, f32[140288]{0:T(1024)}, u32[]{:S(2)}, u32[]{:S(2)}) collective-permute-start(f32[140288]{0:T(1024)} %add_multiply_fusion), channel_id=1, source_target_pairs={{0,1},{1,0},{2,3},{3,2},{4,5},{5,4},{6,7},{7,6},{8,9},{9,8},{10,11... | collective-permute-start | bytes 1683464 | tf_op jit(solution)/shard_map/ppermute | solution.py:448
  (143 other events, 1913.7 us)
